TPU v7x, 32 devices: a whole 2x2x4 slice. The times are simulated.
32 devices in a mesh: groups: 2 (over y), attn: 4 (over x, core), expert: 4 (over z).
Axes of the slice: x: 2, y: 2, z: 4, core: 2. Of those that a mesh axis runs over, the one named last changes fastest.
Arguments:
- tokens: bfloat16 [1024, 4096], P(('groups', 'attn')), parts along dimension 0, may hold values from -6 to 6
- norm_gain: float32 [4096], replicated, may hold values from 0.1 to 1.9
- query_weight: bfloat16 [4096, 4096], P('attn', 'expert'), may hold values from -0.09375 to 0.09375
- key_weight: bfloat16 [4096, 1024], P('attn', 'expert'), may hold values from -0.09375 to 0.09375
- value_weight: bfloat16 [4096, 1024], P('attn', 'expert'), may hold values from -0.09375 to 0.09375
- out_weight: bfloat16 [4096, 4096], P('attn', 'expert'), may hold values from -0.09375 to 0.09375
- cache_key: bfloat16 [8, 2048, 1024], P(('groups', 'attn'), None, 'expert'), parts along dimension 0, may hold values from -240 to 240
- cache_value: bfloat16 [8, 2048, 1024], P(('groups', 'attn'), None, 'expert'), parts along dimension 0, may hold values from -24 to 24
- block_table: int32 [8, 8], P(('groups', 'attn')), parts along dimension 0, may hold values from 0 to 15
- block_count: int32 [8], P(('groups', 'attn')), parts along dimension 0, may hold values from 1 to 8, 24 in all
- expert_ids: int32 [1024, 2], P(('groups', 'attn')), parts along dimension 0, may hold values from 0 to 3, all different within a row; in each aligned block of 128 rows (0 to 127, 128 to 255, ...) at most 96 rows name the same one
- gate_weights: float32 [1024, 2], P(('groups', 'attn')), parts along dimension 0, may hold values from 1 to 3
- post_gain: float32 [4096], replicated, may hold values from 0.1 to 1.9
- expert_gate: bfloat16 [4, 4096, 6400], P('expert', None, 'attn'), may hold values from -0.09375 to 0.09375
- expert_up: bfloat16 [4, 4096, 6400], P('expert', None, 'attn'), may hold values from -0.09375 to 0.09375
- expert_down: bfloat16 [4, 6400, 4096], P('expert', 'attn'), may hold values from -0.15625 to 0.15625
Outputs:
- mixed: bfloat16 [1024, 4096], P(('groups', 'attn'), 'expert'), parts along dimension 0
There are 2 independent parts, one for each index of `groups`. A program takes and returns all parts, laid end to end along the dimension named above; an argument that names none is the same for every part. Nothing has to cross between parts.
Inputs may be any that keep to these rules, and one draw needn't show every extreme that they name: `expert_ids`: in each aligned block of 128 tokens (one sequence) no expert is named more than 96 times; the two ids of a token differ. `block_count`: the counts of one part sum to 24.
All inputs are finite; a program needn't handle non-finite values. No bound on the sum of `block_count` on one device may be relied on, other than what follows from the above.
Results may differ from a plain program's by a relative error of at most 0.02.
Values may be sent and summed in bfloat16 or wider, within the bound.
A program may use at most 128 MiB of HBM per device.

v0:
```python
import math

import jax
import jax.numpy as jnp
from jax import lax
from jax.sharding import PartitionSpec as P

HD = 128
CACHE_BLOCKS = 16
NSEL = 8
BLK = 128


epsilon = 1e-05
rope_base = 10000.0


def layer_norm(values, gain_vector):
    center = jnp.mean(values, axis=-1, keepdims=True)
    spread = jnp.mean(jnp.square(values - center), axis=-1, keepdims=True)
    return (values - center) * lax.rsqrt(spread + epsilon) * gain_vector


def rotate(values, positions, head_size):
    row_count = values.shape[0]
    head_count = values.shape[1] // head_size
    half_size = head_size // 2
    frequency = jnp.exp(
        jnp.arange(half_size, dtype=jnp.float32) * (-2.0 * math.log(rope_base) / head_size)
    )
    angle_table = positions[:, None] * frequency[None, :]
    cosine = jnp.cos(angle_table)[:, None, :]
    sine_part = jnp.sin(angle_table)[:, None, :]
    split_heads = values.reshape(row_count, head_count, head_size)
    first_half = split_heads[..., :half_size]
    second_half = split_heads[..., half_size:]
    turned = jnp.concatenate(
        [
            first_half * cosine - second_half * sine_part,
            second_half * cosine + first_half * sine_part,
        ],
        axis=-1,
    )
    return turned.reshape(row_count, head_count * head_size)


def pair_slots(expert_ids, expert_total):
    flat_ids = expert_ids.reshape(-1)
    onehot = (flat_ids[:, None] == jnp.arange(expert_total, dtype=jnp.int32)[None, :]).astype(
        jnp.int32
    )
    earlier = jnp.cumsum(onehot, axis=0) - onehot
    return jnp.sum(onehot * earlier, axis=1).reshape(expert_ids.shape)


def shards(
    tokens,
    norm_gain,
    query_weight,
    key_weight,
    value_weight,
    out_weight,
    cache_key,
    cache_value,
    block_table,
    block_count,
    expert_ids,
    gate_weights,
    post_gain,
    expert_gate,
    expert_up,
    expert_down,
):
    expert_axis_size = lax.axis_size("expert")
    expert_index = lax.axis_index("expert")
    row_count = tokens.shape[0]
    model_width = tokens.shape[1]
    share_width = model_width // expert_axis_size
    expert_total = expert_axis_size * expert_gate.shape[0]
    capacity = 3 * row_count // expert_total
    query_columns = query_weight.shape[1]
    key_columns = key_weight.shape[1]
    normed = layer_norm(tokens.astype(jnp.float32), norm_gain).astype(jnp.bfloat16)
    stacked = jnp.concatenate([query_weight, key_weight, value_weight], axis=1)
    spread_rows = lax.all_to_all(normed, "attn", split_axis=1, concat_axis=0, tiled=True)
    projected = lax.psum_scatter(
        jnp.dot(spread_rows, stacked, preferred_element_type=jnp.float32),
        "attn",
        scatter_dimension=0,
        tiled=True,
    )
    query_raw = projected[:, :query_columns]
    key_raw = projected[:, query_columns : query_columns + key_columns]
    value_raw = projected[:, query_columns + key_columns :]
    live_blocks = block_count[0]
    row_range = jnp.arange(row_count, dtype=jnp.int32)
    positions = (live_blocks * BLK + row_range).astype(jnp.float32)
    query = rotate(query_raw, positions, HD).astype(jnp.bfloat16)
    key_new = rotate(key_raw, positions, HD).astype(jnp.bfloat16)
    value_new = value_raw.astype(jnp.bfloat16)
    key_heads = key_columns // HD
    group_size = query_columns // key_columns
    score_scale = 1.0 / math.sqrt(HD)
    queries = query.reshape(row_count, key_heads, group_size, HD)
    fresh_keys = key_new.reshape(row_count, key_heads, HD)
    fresh_values = value_new.reshape(row_count, key_heads, HD)
    causal = row_range[:, None] >= row_range[None, :]
    fresh_scores = jnp.where(
        causal,
        jnp.einsum("rkgd,nkd->kgrn", queries, fresh_keys, preferred_element_type=jnp.float32)
        * score_scale,
        -jnp.inf,
    )
    picked_keys = jnp.take(
        cache_key[0].reshape(CACHE_BLOCKS, BLK, key_columns), block_table[0], axis=0
    )
    picked_values = jnp.take(
        cache_value[0].reshape(CACHE_BLOCKS, BLK, key_columns), block_table[0], axis=0
    )
    flat_keys = picked_keys.reshape(NSEL * BLK, key_heads, HD)
    flat_values = picked_values.reshape(NSEL * BLK, key_heads, HD)
    live_keys = jnp.arange(NSEL * BLK, dtype=jnp.int32) // BLK < live_blocks
    cache_scores = jnp.where(
        live_keys,
        jnp.einsum("rkgd,nkd->kgrn", queries, flat_keys, preferred_element_type=jnp.float32)
        * score_scale,
        -jnp.inf,
    )
    largest = jnp.maximum(
        jnp.max(cache_scores, axis=-1, keepdims=True), jnp.max(fresh_scores, axis=-1, keepdims=True)
    )
    cache_exp = jnp.exp(cache_scores - largest)
    fresh_exp = jnp.exp(fresh_scores - largest)
    denominator = jnp.sum(cache_exp, axis=-1, keepdims=True) + jnp.sum(
        fresh_exp, axis=-1, keepdims=True
    )
    context = jnp.einsum(
        "kgrn,nkd->rkgd",
        (cache_exp / denominator).astype(jnp.bfloat16),
        flat_values,
        preferred_element_type=jnp.float32,
    )
    context = context + jnp.einsum(
        "kgrn,nkd->rkgd",
        (fresh_exp / denominator).astype(jnp.bfloat16),
        fresh_values,
        preferred_element_type=jnp.float32,
    )
    context = context.reshape(row_count, query_columns).astype(jnp.bfloat16)
    partial_heads = lax.dot_general(
        lax.all_gather(context, "attn", axis=0, tiled=True),
        out_weight,
        (((1,), (1,)), ((), ())),
        preferred_element_type=jnp.float32,
    )
    by_rows = lax.all_to_all(partial_heads, "attn", split_axis=0, concat_axis=1, tiled=True)
    attended = lax.psum(by_rows, "expert")
    state = (tokens.astype(jnp.float32) + attended).astype(jnp.bfloat16)
    post_normed = layer_norm(state.astype(jnp.float32), post_gain).astype(jnp.bfloat16)
    state_share = lax.dynamic_slice_in_dim(state, expert_index * share_width, share_width, 1)
    slots = pair_slots(expert_ids, expert_total)
    slot_range = jnp.arange(capacity, dtype=jnp.int32)
    picks = [
        (expert_ids[:, pick] == expert_index)[None, :]
        & (slot_range[:, None] == slots[:, pick][None, :])
        for pick in range(2)
    ]
    dispatch_matrix = (picks[0] | picks[1]).astype(jnp.bfloat16)
    buffer = jnp.dot(dispatch_matrix, post_normed, preferred_element_type=jnp.float32).astype(
        jnp.bfloat16
    )
    gate_local = expert_gate[0]
    up_local = expert_up[0]
    down_local = expert_down[0]
    piece = lax.all_gather(buffer, "attn", axis=0, tiled=True)
    gated = jnp.dot(piece, gate_local, preferred_element_type=jnp.float32)
    lifted = jnp.dot(piece, up_local, preferred_element_type=jnp.float32)
    activated = (jax.nn.silu(gated) * lifted).astype(jnp.bfloat16)
    expert_out = lax.psum_scatter(
        jnp.dot(activated, down_local, preferred_element_type=jnp.float32).astype(jnp.bfloat16),
        "attn",
        scatter_dimension=0,
        tiled=True,
    )
    first_term = gate_weights[:, 0:1] * jnp.dot(
        picks[0].T.astype(jnp.bfloat16), expert_out, preferred_element_type=jnp.float32
    )
    second_term = gate_weights[:, 1:2] * jnp.dot(
        picks[1].T.astype(jnp.bfloat16), expert_out, preferred_element_type=jnp.float32
    )
    mixture = lax.psum_scatter(first_term + second_term, "expert", scatter_dimension=1, tiled=True)
    return (state_share.astype(jnp.float32) + mixture).astype(jnp.bfloat16)


def solution(mesh):
    return jax.shard_map(
        shards,
        mesh=mesh,
        in_specs=(
            P(("groups", "attn"), None),
            P(),
            P("attn", "expert"),
            P("attn", "expert"),
            P("attn", "expert"),
            P("attn", "expert"),
            P(("groups", "attn"), None, "expert"),
            P(("groups", "attn"), None, "expert"),
            P(("groups", "attn"), None),
            P(("groups", "attn")),
            P(("groups", "attn"), None),
            P(("groups", "attn"), None),
            P(),
            P("expert", None, "attn"),
            P("expert", None, "attn"),
            P("expert", "attn", None),
        ),
        out_specs=P(("groups", "attn"), "expert"),
        check_vma=False,
    )
```

profile of v0, /device:TPU:0, one launch (start us, length us, event | category | flops | bytes accessed | tf_op | source)
XLA Modules:
  0.0 385.7 jit_solution(5434945868613635034)
XLA Ops:
  6.5 1.6 convert_reduce_fusion
  8.2 1.7 fusion.28
  9.8 1.1 fusion.30
  11.0 0.1 copy.88
  11.1 18.7 %all_to_all.38 = bf16[128,4,1024]{2,0,1:T(8,128)(2,1)S(1)} all-to-all(bf16[128,4,1024]{2,0,1:T(8,128)(2,1)S(1)} %bitcast.112), channel_id=1, replica_groups=mesh['groups'=2,'attn'=4,'expert'=4] {'attn'}, dimensions={1} | all-to-all | bytes 2097152 | tf_op jit(solution)/shard_map/all_to_all | solution.py:85
  29.8 3.5 fusion.12
  33.3 0.0 all-gather.3.cloned.1.call-start
  34.0 2.6 gather_fusion
  36.7 2.6 gather_fusion.1
  39.3 2.4 broadcast_select_fusion.1
  41.7 2.1 reshape.199
  43.7 2.0 reshape.198
  45.7 0.5 fusion.68
  46.3 0.3 multiply_cosine_fusion
  46.6 25.1 %reduce-scatter.4.cloned.1.call-done = f32[128,1536]{1,0:T(8,128)} async-done(((f32[512,1536]{1,0:T(8,128)}), f32[128,1536]{1,0:T(8,128)}) %reduce-scatter.4.cloned.1.call-update) | async-done | bytes 786448 | tf_op jit(solution)/shard_map/reduce_scatter | solution.py:86
  71.8 1.1 slice_bitcast_fusion
  72.8 0.1 copy.74
  72.9 0.3 subtract_convert_fusion
  73.2 0.1 pad_maximum_fusion
  73.4 1.6 slice.68
  75.0 1.0 reshape.168
  76.0 0.2 fusion.81
  76.2 0.9 subtract_convert_fusion.1
  77.1 1.8 bitcast_reduce_fusion
  78.9 0.3 fusion.82
  79.2 1.0 copy-done.6
  80.3 0.1 fusion.48
  80.4 0.9 fusion.11
  81.3 0.9 slice.87
  82.2 0.1 copy.69
  82.4 3.6 fusion.35
  86.0 1.0 fusion.38
  87.0 0.0 all-gather.3.cloned.1.call-update
  87.0 0.0 all-reduce.2.cloned.1.call-start
  87.1 16.9 %all-gather.3.cloned.1.call-done = bf16[512,1024]{0,1:T(8,128)(2,1)} async-done(((bf16[128,1024]{0,1:T(8,128)(2,1)}), bf16[512,1024]{0,1:T(8,128)(2,1)}) %all-gather.3.cloned.1.call-update) | async-done | bytes 1048592 | tf_op jit(solution)/shard_map/all_gather | solution.py:151
  104.0 2.5 fusion.83
  106.5 28.2 %all_to_all.39 = f32[4,128,1024]{2,1,0:T(8,128)S(1)} all-to-all(f32[4,128,1024]{2,1,0:T(8,128)S(1)} %bitcast.116), channel_id=1, replica_groups=mesh['groups'=2,'attn'=4,'expert'=4] {'attn'}, dimensions={0} | all-to-all | bytes 4194304 | tf_op jit(solution)/shard_map/all_to_all | solution.py:156
  134.7 1.5 copy.73
  136.3 0.0 all-gather.5.cloned.1.call-start
  136.3 0.1 copy.52
  136.4 0.1 eq.87
  136.6 0.1 eq.83
  136.7 1.2 reduce-window.6
  138.0 0.1 slice.72
  138.0 0.1 copy.54
  138.2 0.1 copy.55
  138.3 0.1 add_bitcast_fusion
  138.4 0.1 reshape.171
  138.5 0.2 slice_reduce_fusion.1
  138.7 84.2 %all-reduce.2.cloned.1.call-done = f32[128,4096]{1,0:T(8,128)} async-done(((f32[128,4096]{1,0:T(8,128)}), f32[128,4096]{1,0:T(8,128)}) %all-reduce.2.cloned.1.call-update) | async-done | bytes 2097168 | tf_op jit(solution)/shard_map/psum | solution.py:157
  222.9 1.9 convert_reduce_fusion.1
  224.9 0.4 fusion.31
  225.3 1.5 convolution_convert_fusion
  226.8 0.0 reduce-scatter.6.cloned.1.call-start
  226.9 27.6 %all-gather.5.cloned.1.call-done = bf16[384,4096]{1,0:T(8,128)(2,1)} async-done(((bf16[96,4096]{1,0:T(8,128)(2,1)}), bf16[384,4096]{1,0:T(8,128)(2,1)}) %all-gather.5.cloned.1.call-update) | async-done | bytes 3145744 | tf_op jit(solution)/shard_map/all_gather | solution.py:175
  254.5 12.0 %fusion.4 = f32[384,1600]{0,1:T(8,128)} fusion(bf16[384,4096]{1,0:T(8,128)(2,1)} %all-gather.5.cloned.1.call-done, bf16[1,4096,1600]{1,2,0:T(8,128)(2,1)} %param.31), kind=kOutput, calls=%fused_computation.6 | convolution fusion | flops 5033164800 | bytes 18710528 | tf_op jit(solution)/shard_map/dot_general | solution.py:176
  266.5 24.7 %fusion.6 = bf16[384,4096]{1,0:T(8,128)(2,1)} fusion(bf16[1,1600,4096]{2,1,0:T(8,128)(2,1)} %param.33, bf16[384,4096]{1,0:T(8,128)(2,1)} %all-gather.5.cloned.1.call-done, bf16[1,4096,1600]{1,2,0:T(8,128)(2,1)} %param.32, f32[384,1600]{0,1:T(8,128)} %fusion.4), kind=kOutput, calls=%fused_computation.8 | convolution fusion | flops 10071588864 | bytes 34963456 | tf_op jit(solution)/shard_map/dot_general | solution.py:180
  291.2 0.0 reduce-scatter.8.cloned.1.call-start
  291.3 0.6 copy-done.12
  291.9 37.5 %reduce-scatter.6.cloned.1.call-done = bf16[96,4096]{1,0:T(8,128)(2,1)} async-done(((bf16[384,4096]{1,0:T(8,128)(2,1)}), bf16[96,4096]{1,0:T(8,128)(2,1)}) %reduce-scatter.6.cloned.1.call-update) | async-done | bytes 786448 | tf_op jit(solution)/shard_map/reduce_scatter | solution.py:179
  329.3 1.7 convolution_multiply_fusion.1
  331.0 1.8 fusion.9
  332.9 44.0 %reduce-scatter.8.cloned.1.call-done = f32[128,1024]{1,0:T(8,128)} async-done(((f32[128,4096]{1,0:T(8,128)}), f32[128,1024]{1,0:T(8,128)}) %reduce-scatter.8.cloned.1.call-update) | async-done | bytes 524304 | tf_op jit(solution)/shard_map/reduce_scatter | solution.py:191
  376.9 1.9 add_convert_fusion
  (59 shorter events, 0.4 us)
Async XLA Ops:
  6.5 97.5 %copy-start = (bf16[1024,1024]{1,0:T(8,128)(2,1)S(1)}, bf16[1024,1024]{1,0:T(8,128)(2,1)}, u32[]{:S(2)}) copy-start(bf16[1024,1024]{1,0:T(8,128)(2,1)} %param.23) | copy-start | bytes 6291460
  6.5 3.3 copy-start.3
  6.5 65.2 %reduce-scatter.4.cloned.1.call-start = ((), (), s32[]{:S(2)}) async-start(), calls=%async_computation.5 | async-start | bytes 3932160 | tf_op jit(solution)/shard_map/reduce_scatter | solution.py:86
  10.9 18.9 %copy-start.13 = (bf16[1024,1024]{1,0:T(8,128)(2,1)S(1)}, bf16[1024,1024]{1,0:T(8,128)(2,1)}, u32[]{:S(2)}) copy-start(bf16[1024,1024]{1,0:T(8,128)(2,1)} %param.20) | copy-start | bytes 6291460
  11.0 18.9 %copy-start.14 = (bf16[1024,256]{1,0:T(8,128)(2,1)S(1)}, bf16[1024,256]{1,0:T(8,128)(2,1)}, u32[]{:S(2)}) copy-start(bf16[1024,256]{1,0:T(8,128)(2,1)} %param.22) | copy-start | bytes 1572868
  11.0 18.8 %copy-start.15 = (bf16[1024,256]{1,0:T(8,128)(2,1)S(1)}, bf16[1024,256]{1,0:T(8,128)(2,1)}, u32[]{:S(2)}) copy-start(bf16[1024,256]{1,0:T(8,128)(2,1)} %param.21) | copy-start | bytes 1572868
  33.3 0.7 copy-start.17
  33.3 70.7 %all-gather.3.cloned.1.call-start = ((), (), s32[]{:S(2)}) async-start(), calls=%async_computation.6 | async-start | bytes 1310720 | tf_op jit(solution)/shard_map/all_gather | solution.py:151
  46.6 26.6 %copy-start.8 = (f32[128,64]{1,0:T(8,128)}, f32[128,64]{1,0:T(8,128)S(1)}, u32[]{:S(2)}) copy-start(f32[128,64]{1,0:T(8,128)S(1)} %get-tuple-element.20) | copy-start | bytes 98308
  46.6 26.6 %copy-start.9 = (f32[128,64]{1,0:T(8,128)}, f32[128,64]{1,0:T(8,128)S(1)}, u32[]{:S(2)}) copy-start(f32[128,64]{1,0:T(8,128)S(1)} %get-tuple-element.21) | copy-start | bytes 98308
  77.1 3.2 copy-start.10
  78.9 2.4 copy-start.2
  79.2 1.1 copy-start.6
  82.4 3.7 copy-start.7
  87.0 135.9 %all-reduce.2.cloned.1.call-start = ((), (), s32[]{:S(2)}) async-start(), calls=%async_computation.7 | async-start | bytes 4194304 | tf_op jit(solution)/shard_map/psum | solution.py:157
  134.7 1.6 copy-start.11
  136.3 118.2 %all-gather.5.cloned.1.call-start = ((), (), s32[]{:S(2)}) async-start(), calls=%async_computation.8 | async-start | bytes 3932160 | tf_op jit(solution)/shard_map/all_gather | solution.py:175
  138.7 86.6 %copy-start.16 = (f32[4096]{0:T(1024)S(1)}, f32[4096]{0:T(1024)}, u32[]{:S(2)}) copy-start(f32[4096]{0:T(1024)} %param.30) | copy-start | bytes 49156
  224.9 41.6 %copy-start.4 = (bf16[128,4096]{1,0:T(8,128)(2,1)}, bf16[128,4096]{1,0:T(8,128)(2,1)S(1)}, u32[]{:S(2)}) copy-start(bf16[128,4096]{1,0:T(8,128)(2,1)S(1)} %get-tuple-element.9) | copy-start | bytes 3145732
  226.8 102.5 %reduce-scatter.6.cloned.1.call-start = ((), (), s32[]{:S(2)}) async-start(), calls=%async_computation.9 | async-start | bytes 3932160 | tf_op jit(solution)/shard_map/reduce_scatter | solution.py:179
  291.2 0.7 copy-start.12
  291.2 85.7 %reduce-scatter.8.cloned.1.call-start = ((), (), s32[]{:S(2)}) async-start(), calls=%async_computation.10 | async-start | bytes 2621440 | tf_op jit(solution)/shard_map/reduce_scatter | solution.py:191
  329.3 1.7 copy-start.5
  331.0 47.8 %copy-start.1 = (bf16[1024,1024]{1,0:T(8,128)(2,1)S(1)}, bf16[1024,1024]{1,0:T(8,128)(2,1)}, u32[]{:S(2)}) copy-start(bf16[1024,1024]{1,0:T(8,128)(2,1)} %param.23) | copy-start | bytes 6291460
Sparse Core Ops, SparseCore 0:
  33.4 38.2 reduce-scatter.3
  87.1 16.8 all-gather.2
  136.4 86.4 all-reduce.1
  227.0 27.4 all-gather.4
  291.3 37.9 reduce-scatter.5
  333.0 43.8 reduce-scatter.7
where the time goes:
time: 386 us
  waiting for transfers between devices  235 us (61%)
  matrix products  54.4 us (14%)
  blocking collectives  46.9 us (12%)
  local copies, waits for them, and re-layouts  18.6 us (5%)
  other arithmetic  15.6 us (4%)
  between operations  14.5 us (4%)
    psum x1, waiting for transfers between devices, shards(): attended = lax.psum(by_rows, 'expert')  84.2 us
    reduce_scatter x1, waiting for transfers between devices, shards(): lax.psum_scatter(first_term + second_term, 'expert', scatter_dimension=1,...  44 us
    reduce_scatter x1, waiting for transfers between devices, shards(): lax.psum_scatter(jnp.dot(activated, down_local, preferred_element_type=jn...  37.5 us
    all_to_all x1, blocking collectives, shards(): lax.all_to_all(partial_heads, 'attn', split_axis=0, concat_axis=1, tiled=...  28.2 us
    all_gather x1, waiting for transfers between devices, shards(): piece = lax.all_gather(buffer, 'attn', axis=0, tiled=True)  27.6 us
    reduce_scatter x1, waiting for transfers between devices, shards(): lax.psum_scatter(jnp.dot(spread_rows, stacked, preferred_element_type=jnp...  25.1 us
    dot_general x1, matrix products, shards(): jnp.dot(activated, down_local, preferred_element_type=jnp.float32)  24.7 us
    all_to_all x1, blocking collectives, shards(): lax.all_to_all(normed, 'attn', split_axis=1, concat_axis=0, tiled=True)  18.7 us
  transfers between devices with their start and end apart: 6, of which 6 were waited for; matrix products, arithmetic and copies ran while one was open for 4% of the time, Pallas kernels for 0%

commit v1 on v0

v1 whole, which is shorter than its diff:
```python
import functools
import math

import jax
import jax.numpy as jnp
from jax import lax
from jax.experimental import pallas as pl
from jax.experimental.pallas import tpu as pltpu
from jax.sharding import PartitionSpec as P

HD = 128
BLK = 128
TILE = 256
LAG = 4
TRANSPOSED = (((1,), (1,)), ((), ()))
MESH = pl.DeviceIdType.MESH


epsilon = 1e-05
rope_base = 10000.0


def pair_slots(expert_ids, expert_total):
    flat_ids = expert_ids.reshape(-1)
    onehot = (flat_ids[:, None] == jnp.arange(expert_total, dtype=jnp.int32)[None, :]).astype(
        jnp.int32
    )
    earlier = jnp.cumsum(onehot, axis=0) - onehot
    return jnp.sum(onehot * earlier, axis=1).reshape(expert_ids.shape)


def moe_kernel(
    chips,
    depth,
    buffer_ref,
    gate_ref,
    up_ref,
    down_ref,
    picks_ref,
    weights_ref,
    out_ref,
    gate_all,
    up_all,
    down_all,
    piece,
    activated,
    partial,
    keep,
    pair_send,
    pair_recv,
    chip_send,
    chip_recv,
    mine,
    mix_send,
    mix_recv,
    load_sem,
    gather_send,
    forward_send,
    gather_recv,
    pair_send_sem,
    pair_recv_sem,
    chip_send_sem,
    chip_recv_sem,
    mix_send_sem,
    mix_recv_sem,
):
    me = lax.axis_index("attn")
    expert = lax.axis_index("expert")
    chip = me // 2
    core = me % 2
    partner = me + 1 - 2 * core
    capacity = buffer_ref.shape[0]
    hidden = activated.shape[1]
    steps = pair_send.shape[0]
    width = partial.shape[1]
    per_owner = steps // depth
    loads = [
        pltpu.make_async_copy(source.at[0], target, load_sem.at[i])
        for i, (source, target) in enumerate(
            [(gate_ref, gate_all), (up_ref, up_all), (down_ref, down_all)]
        )
    ]
    for load in loads:
        load.start()

    def other_chip(k):
        return lax.rem(chip + k, chips)

    def other_expert(k):
        return lax.rem(expert + k, depth)

    barrier = pltpu.get_barrier_semaphore()
    pl.semaphore_signal(barrier, inc=1, device_id={"attn": partner}, device_id_type=MESH)
    for k in range(1, chips):
        pl.semaphore_signal(
            barrier, inc=1, device_id={"attn": other_chip(k) * 2 + core}, device_id_type=MESH
        )
    for k in range(1, depth):
        pl.semaphore_signal(
            barrier, inc=1, device_id={"expert": other_expert(k)}, device_id_type=MESH
        )
    pl.semaphore_wait(barrier, chips + depth - 1)

    def seq_rows(seq, count=1):
        return pl.ds(pl.multiple_of(seq * capacity, 16), count * capacity)

    def send(source, target, send_sem, recv_sem, where):
        return pltpu.make_async_remote_copy(
            src_ref=source,
            dst_ref=target,
            send_sem=send_sem,
            recv_sem=recv_sem,
            device_id=where,
            device_id_type=MESH,
        )

    def gather_copy(k):
        where = {"attn": partner} if k == 0 else {"attn": other_chip(k) * 2 + core}
        return send(
            buffer_ref, piece.at[seq_rows(me)], gather_send.at[k], gather_recv.at[me], where
        )

    def forward_copy(k):
        seq = other_chip(k) * 2 + core
        return send(
            piece.at[seq_rows(seq)],
            piece.at[seq_rows(seq)],
            forward_send.at[k],
            gather_recv.at[seq],
            {"attn": partner},
        )

    def arrival(seq):
        return send(
            buffer_ref,
            piece.at[seq_rows(seq)],
            gather_send.at[0],
            gather_recv.at[seq],
            {"attn": partner},
        )

    for k in range(1, chips):
        gather_copy(k).start()
    gather_copy(0).start()
    piece[seq_rows(me), :] = buffer_ref[...]

    def hidden_tile(rows, start, size):
        values = piece[rows, :]
        columns = pl.ds(start, size)
        gated = lax.dot_general(
            values, gate_all[columns, :], TRANSPOSED, preferred_element_type=jnp.float32
        )
        lifted = lax.dot_general(
            values, up_all[columns, :], TRANSPOSED, preferred_element_type=jnp.float32
        )
        activated[rows, columns] = (jax.nn.silu(gated) * lifted).astype(jnp.bfloat16)

    for k in range(chips):
        if k == 0:
            arrival(partner).wait_recv()
            loads[0].wait()
            loads[1].wait()
        else:
            seq = other_chip(k) * 2 + core
            arrival(seq).wait_recv()
            forward_copy(k).start()
            arrival(other_chip(k) * 2 + 1 - core).wait_recv()
        rows = seq_rows(other_chip(k) * 2, 2)
        full = hidden // TILE

        def tile_body(tile, carry):
            hidden_tile(rows, pl.multiple_of(tile * TILE, TILE), TILE)
            return carry

        lax.fori_loop(0, full, tile_body, 0)
        if hidden % TILE:
            hidden_tile(rows, full * TILE, hidden % TILE)
    loads[2].wait()

    def owner_of(step):
        return lax.rem(expert + 1 + step // per_owner, depth)

    def pair_copy(step):
        return send(
            pair_send.at[step],
            pair_recv.at[step],
            pair_send_sem.at[step],
            pair_recv_sem.at[step],
            {"attn": partner},
        )

    def chip_copy(step, k):
        return send(
            chip_send.at[step, k],
            chip_recv.at[step, chip],
            chip_send_sem.at[step, k],
            chip_recv_sem.at[step, chip],
            {"attn": other_chip(k) * 2 + core},
        )

    def chip_arrival(step, k):
        return send(
            chip_send.at[step, k],
            chip_recv.at[step, other_chip(k)],
            chip_send_sem.at[step, k],
            chip_recv_sem.at[step, other_chip(k)],
            {"attn": other_chip(k) * 2 + core},
        )

    def mix_copy(step):
        return send(
            mix_send.at[step],
            mix_recv.at[expert, lax.rem(step, per_owner)],
            mix_send_sem.at[step],
            mix_recv_sem.at[expert, lax.rem(step, per_owner)],
            {"expert": owner_of(step)},
        )

    def mix_arrival(source, part):
        return send(
            mix_send.at[0],
            mix_recv.at[source, part],
            mix_send_sem.at[0],
            mix_recv_sem.at[source, part],
            {"expert": source},
        )

    def project(step):
        columns = pl.ds(
            pl.multiple_of((owner_of(step) * per_owner + lax.rem(step, per_owner)) * width, width),
            width,
        )
        partial[...] = jnp.dot(
            activated[...], down_all[:, columns], preferred_element_type=jnp.float32
        )
        for k in range(chips):
            keep[lax.rem(step, 2), k] = partial[seq_rows(other_chip(k) * 2 + core), :]
            pair_send[step, other_chip(k)] = partial[
                seq_rows(other_chip(k) * 2 + 1 - core), :
            ].astype(jnp.bfloat16)
        pair_copy(step).start()

    def pair_sum(step):
        pair_copy(step).wait_recv()
        for k in range(chips):
            both = keep[lax.rem(step, 2), k] + pair_recv[step, other_chip(k)].astype(jnp.float32)
            if k == 0:
                mine[step] = both
            else:
                chip_send[step, k] = both.astype(jnp.bfloat16)
                chip_copy(step, k).start()

    def combine(step):
        total = mine[step]
        for k in range(1, chips):
            chip_arrival(step, k).wait_recv()
            total = total + chip_recv[step, other_chip(k)].astype(jnp.float32)
        expert_out = total.astype(jnp.bfloat16)
        mixture = weights_ref[:, 0:1] * jnp.dot(
            picks_ref[0], expert_out, preferred_element_type=jnp.float32
        ) + weights_ref[:, 1:2] * jnp.dot(
            picks_ref[1], expert_out, preferred_element_type=jnp.float32
        )
        part = lax.rem(step, per_owner)

        @pl.when(step < steps - per_owner)
        def _():
            mix_send[step] = mixture.astype(jnp.bfloat16)
            mix_copy(step).start()

        @pl.when(step >= steps - per_owner)
        def _():
            out_ref[part] = mixture

    def step_body(step, carry):
        @pl.when(step < steps)
        def _():
            project(step)

        @pl.when((step >= 1) & (step <= steps))
        def _():
            pair_sum(step - 1)

        @pl.when(step >= LAG)
        def _():
            combine(step - LAG)

        return carry

    lax.fori_loop(0, steps + LAG, step_body, 0)

    for part in range(per_owner):
        total = out_ref[part]
        for k in range(1, depth):
            mix_arrival(other_expert(k), part).wait_recv()
            total = total + mix_recv[other_expert(k), part].astype(jnp.float32)
        out_ref[part] = total

    for k in range(chips):
        gather_copy(k).wait_send()
    for k in range(1, chips):
        forward_copy(k).wait_send()
    def finish(step, carry):
        pair_copy(step).wait_send()
        for k in range(1, chips):
            chip_copy(step, k).wait_send()

        @pl.when(step < steps - per_owner)
        def _():
            mix_copy(step).wait_send()

        return carry

    lax.fori_loop(0, steps, finish, 0)


def expert_layer(buffer, gate, up, down, picks, weights):
    n = lax.axis_size("attn")
    depth = lax.axis_size("expert")
    chips = n // 2
    capacity, model_width = buffer.shape
    hidden = gate.shape[2]
    row_count = weights.shape[0]
    share = model_width // depth
    width = math.gcd(share, 512)
    per_owner = share // width
    steps = model_width // width
    vmem = pl.BlockSpec(memory_space=pltpu.VMEM)
    anywhere = pl.BlockSpec(memory_space=pl.ANY)
    dma = pltpu.SemaphoreType.DMA
    out = pl.pallas_call(
        functools.partial(moe_kernel, chips, depth),
        out_shape=jax.ShapeDtypeStruct((per_owner, row_count, width), jnp.float32),
        in_specs=[vmem, anywhere, anywhere, anywhere, vmem, vmem],
        out_specs=vmem,
        scratch_shapes=[
            pltpu.VMEM((hidden, model_width), jnp.bfloat16),
            pltpu.VMEM((hidden, model_width), jnp.bfloat16),
            pltpu.VMEM((hidden, model_width), jnp.bfloat16),
            pltpu.VMEM((n * capacity, model_width), jnp.bfloat16),
            pltpu.VMEM((n * capacity, hidden), jnp.bfloat16),
            pltpu.VMEM((n * capacity, width), jnp.float32),
            pltpu.VMEM((2, chips, capacity, width), jnp.float32),
            pltpu.VMEM((steps, chips, capacity, width), jnp.bfloat16),
            pltpu.VMEM((steps, chips, capacity, width), jnp.bfloat16),
            pltpu.VMEM((steps, chips, capacity, width), jnp.bfloat16),
            pltpu.VMEM((steps, chips, capacity, width), jnp.bfloat16),
            pltpu.VMEM((steps, capacity, width), jnp.float32),
            pltpu.VMEM((steps, row_count, width), jnp.bfloat16),
            pltpu.VMEM((depth, per_owner, row_count, width), jnp.bfloat16),
            dma((3,)),
            dma((chips,)),
            dma((chips,)),
            dma((n,)),
            dma((steps,)),
            dma((steps,)),
            dma((steps, chips)),
            dma((steps, chips)),
            dma((steps,)),
            dma((depth, per_owner)),
        ],
        compiler_params=pltpu.CompilerParams(
            collective_id=0, has_side_effects=True, vmem_limit_bytes=63 * 1024 * 1024
        ),
        cost_estimate=pl.CostEstimate(
            flops=6 * n * capacity * model_width * hidden,
            bytes_accessed=6 * model_width * hidden,
            transcendentals=n * capacity * hidden,
        ),
    )(buffer, gate.swapaxes(1, 2), up.swapaxes(1, 2), down, picks, weights)
    return out.transpose(1, 0, 2).reshape(row_count, share)


def listed_kernel(table_ref, cache_key_ref, cache_value_ref, keys_ref, values_ref, sems):
    copies = []
    for j in range(table_ref.shape[1]):
        source = pl.ds(pl.multiple_of(table_ref[0, j] * BLK, BLK), BLK)
        target = pl.ds(j * BLK, BLK)
        for i, (cache, listed) in enumerate(
            [(cache_key_ref, keys_ref), (cache_value_ref, values_ref)]
        ):
            copies.append(
                pltpu.make_async_copy(cache.at[0, source], listed.at[target], sems.at[i, j])
            )
    for copy in copies:
        copy.start()
    for copy in copies:
        copy.wait()


def listed_blocks(block_table, cache_key, cache_value):
    listed = block_table.shape[1]
    shape = jax.ShapeDtypeStruct((listed * BLK, cache_key.shape[2]), cache_key.dtype)
    vmem = pl.BlockSpec(memory_space=pltpu.VMEM)
    anywhere = pl.BlockSpec(memory_space=pl.ANY)
    return pl.pallas_call(
        listed_kernel,
        out_shape=(shape, shape),
        in_specs=[pl.BlockSpec(memory_space=pltpu.SMEM), anywhere, anywhere],
        out_specs=(vmem, vmem),
        scratch_shapes=[pltpu.SemaphoreType.DMA((2, listed))],
    )(block_table, cache_key, cache_value)


def attention_kernel(
    chips,
    depth,
    tokens_ref,
    gain_ref,
    cosine_ref,
    sine_ref,
    bias_ref,
    post_gain_ref,
    dispatch_ref,
    query_weight_ref,
    key_weight_ref,
    value_weight_ref,
    cache_key_ref,
    cache_value_ref,
    out_weight_ref,
    buffer_ref,
    state_ref,
    query_all,
    key_all,
    value_all,
    cache_keys,
    cache_values,
    out_all,
    normed,
    pieces,
    partial,
    keep,
    pair_send,
    pair_recv,
    chip_send,
    chip_recv,
    projected,
    scores,
    contexts,
    head_sums,
    line_send,
    from_left,
    from_right,
    seq_send,
    seq_recv,
    states,
    post,
    load_sem,
    piece_send,
    piece_recv,
    pair_send_sem,
    pair_recv_sem,
    chip_send_sem,
    chip_recv_sem,
    gather_send,
    forward_send,
    gather_recv,
    line_send_sem,
    left_sem,
    right_sem,
    seq_send_sem,
    seq_recv_sem,
    state_right,
    state_left,
    state_recv,
):
    me = lax.axis_index("attn")
    expert = lax.axis_index("expert")
    n = 2 * chips
    chip = me // 2
    core = me % 2
    partner = me + 1 - 2 * core
    row_count, model_width = tokens_ref.shape
    block = model_width // n
    query_columns = query_all.shape[1]
    key_columns = key_all.shape[1]
    part_rows = row_count // depth
    loads = [
        pltpu.make_async_copy(source, target, load_sem.at[i])
        for i, (source, target) in enumerate(
            [
                (query_weight_ref, query_all),
                (key_weight_ref, key_all),
                (value_weight_ref, value_all),
                (cache_key_ref, cache_keys),
                (cache_value_ref, cache_values),
                (out_weight_ref, out_all),
            ]
        )
    ]
    for load in loads:
        load.start()

    def other_chip(k):
        return lax.rem(chip + k, chips)

    def send(source, target, send_sem, recv_sem, where):
        return pltpu.make_async_remote_copy(
            src_ref=source,
            dst_ref=target,
            send_sem=send_sem,
            recv_sem=recv_sem,
            device_id=where,
            device_id_type=MESH,
        )

    def seq_rows(seq, count=1):
        return pl.ds(pl.multiple_of(seq * row_count, row_count), count * row_count)

    barrier = pltpu.get_barrier_semaphore()
    for k in range(1, n):
        pl.semaphore_signal(
            barrier, inc=1, device_id={"attn": lax.rem(me + k, n)}, device_id_type=MESH
        )
    for k in range(1, depth):
        pl.semaphore_signal(
            barrier, inc=1, device_id={"expert": lax.rem(expert + k, depth)}, device_id_type=MESH
        )

    def norm(values, gain):
        center = jnp.mean(values, axis=-1, keepdims=True)
        spread = jnp.mean(jnp.square(values - center), axis=-1, keepdims=True)
        return ((values - center) * lax.rsqrt(spread + epsilon) * gain).astype(jnp.bfloat16)

    def norm_rows(i, carry):
        rows = pl.ds(pl.multiple_of(i * 16, 16), 16)
        result = norm(tokens_ref[rows, :].astype(jnp.float32), gain_ref[...])
        for f in range(n):
            normed[f, rows, :] = result[:, f * block : (f + 1) * block]
        return carry

    lax.fori_loop(0, row_count // 16, norm_rows, 0)
    pl.semaphore_wait(barrier, n - 1 + depth - 1)

    def piece_copy(seq):
        return send(
            normed.at[seq],
            pieces.at[seq_rows(me)],
            piece_send.at[seq],
            piece_recv.at[me],
            {"attn": seq},
        )

    def piece_arrival(seq):
        return send(
            normed.at[seq],
            pieces.at[seq_rows(seq)],
            piece_send.at[seq],
            piece_recv.at[seq],
            {"attn": seq},
        )

    for k in range(1, chips):
        piece_copy(other_chip(k) * 2 + core).start()
        piece_copy(other_chip(k) * 2 + 1 - core).start()
    piece_copy(partner).start()
    pieces[seq_rows(me), :] = normed[me]

    def pair_copy(k):
        return send(
            pair_send.at[k],
            pair_recv.at[k],
            pair_send_sem.at[k],
            pair_recv_sem.at[k],
            {"attn": partner},
        )

    def chip_copy(k):
        return send(
            chip_send.at[k],
            chip_recv.at[chip],
            chip_send_sem.at[k],
            chip_recv_sem.at[chip],
            {"attn": other_chip(k) * 2 + core},
        )

    def chip_arrival(k):
        return send(
            chip_send.at[k],
            chip_recv.at[other_chip(k)],
            chip_send_sem.at[k],
            chip_recv_sem.at[other_chip(k)],
            {"attn": other_chip(k) * 2 + core},
        )

    for k in range(chips):
        if k == 0:
            for load in loads[:3]:
                load.wait()
        else:
            piece_arrival(other_chip(k) * 2 + core).wait_recv()
        if k == 0:
            piece_arrival(partner).wait_recv()
        else:
            piece_arrival(other_chip(k) * 2 + 1 - core).wait_recv()
        rows = pieces[seq_rows(other_chip(k) * 2, 2), :]
        start = 0
        for weight in (query_all, key_all, value_all):
            size = weight.shape[1]
            partial[:, start : start + size] = jnp.dot(
                rows, weight[...], preferred_element_type=jnp.float32
            )
            start += size
        keep[k] = partial[seq_rows(core), :]
        pair_send[k] = partial[seq_rows(1 - core), :].astype(jnp.bfloat16)
        pair_copy(k).start()
        if k > 0:
            pair_copy(k).wait_recv()
            chip_send[k] = (keep[k] + pair_recv[k].astype(jnp.float32)).astype(jnp.bfloat16)
            chip_copy(k).start()
    pair_copy(0).wait_recv()
    projected[...] = keep[0] + pair_recv[0].astype(jnp.float32)
    for k in range(1, chips):
        chip_arrival(k).wait_recv()
        projected[...] = projected[...] + chip_recv[other_chip(k)].astype(jnp.float32)

    loads[3].wait()
    loads[4].wait()
    half = HD // 2
    group = query_columns // key_columns

    def turned(start):
        values = projected[:, start : start + HD]
        swapped = jnp.concatenate([values[:, half:], values[:, :half]], axis=1)
        return (values * cosine_ref[...] + swapped * sine_ref[...]).astype(jnp.bfloat16)

    score_scale = 1.0 / math.sqrt(HD)
    listed = bias_ref.shape[0]
    group_rows = group * row_count
    row_of = lax.rem(lax.broadcasted_iota(jnp.int32, (group_rows, row_count), 0), row_count)
    column_of = lax.broadcasted_iota(jnp.int32, (group_rows, row_count), 1)
    causal = row_of >= column_of
    for head in range(key_columns // HD):
        columns = slice(head * HD, (head + 1) * HD)
        queries = jnp.concatenate(
            [turned((head * group + g) * HD) for g in range(group)], axis=0
        )
        fresh_keys = turned(query_columns + head * HD)
        value_start = query_columns + key_columns + head * HD
        fresh_values = projected[:, value_start : value_start + HD].astype(jnp.bfloat16)

        def cache_rows(j):
            return slice(j * BLK, (j + 1) * BLK)

        def score(keys):
            values = lax.dot_general(
                queries, keys, TRANSPOSED, preferred_element_type=jnp.float32
            )
            return values * score_scale

        fresh_scores = jnp.where(causal, score(fresh_keys), -jnp.inf)
        scores[listed] = fresh_scores
        largest = fresh_scores
        for j in range(listed):
            block_scores = score(cache_keys[cache_rows(j), columns]) + bias_ref[j : j + 1, :]
            scores[j] = block_scores
            largest = jnp.maximum(largest, block_scores)
        largest = jnp.max(largest, axis=-1, keepdims=True)
        total = jnp.zeros((group_rows, row_count), jnp.float32)
        for j in range(listed + 1):
            exponent = jnp.exp(scores[j] - largest)
            scores[j] = exponent
            total = total + exponent
        denominator = jnp.sum(total, axis=-1, keepdims=True)
        context = jnp.zeros((group_rows, HD), jnp.float32)
        for j in range(listed + 1):
            values = fresh_values if j == listed else cache_values[cache_rows(j), columns]
            context = context + jnp.dot(
                (scores[j] / denominator).astype(jnp.bfloat16),
                values,
                preferred_element_type=jnp.float32,
            )
        for g in range(group):
            start = (head * group + g) * HD
            contexts[seq_rows(me), start : start + HD] = context[
                g * row_count : (g + 1) * row_count
            ].astype(jnp.bfloat16)

    def gather_copy(k):
        where = {"attn": partner} if k == 0 else {"attn": other_chip(k) * 2 + core}
        return send(
            contexts.at[seq_rows(me)],
            contexts.at[seq_rows(me)],
            gather_send.at[k],
            gather_recv.at[me],
            where,
        )

    def forward_copy(k):
        seq = other_chip(k) * 2 + core
        return send(
            contexts.at[seq_rows(seq)],
            contexts.at[seq_rows(seq)],
            forward_send.at[k],
            gather_recv.at[seq],
            {"attn": partner},
        )

    def gather_arrival(seq):
        return send(
            contexts.at[seq_rows(seq)],
            contexts.at[seq_rows(seq)],
            gather_send.at[0],
            gather_recv.at[seq],
            {"attn": partner},
        )

    for k in range(1, chips):
        gather_copy(k).start()
    gather_copy(0).start()

    def line_copy(k, target, rightward):
        seqs = pl.ds(other_chip(k) * 2, 2)
        return send(
            line_send.at[target, seqs],
            (from_left if rightward else from_right).at[target, seqs],
            line_send_sem.at[target, k],
            (left_sem if rightward else right_sem).at[target, k],
            {"expert": lax.rem(expert + (1 if rightward else depth - 1), depth)},
        )

    def line_add(k, target, rightward):
        seqs = pl.ds(other_chip(k) * 2, 2)
        line_copy(k, target, rightward).wait_recv()
        arrived = (from_left if rightward else from_right)[target, seqs]
        line_send[target, seqs] = (
            line_send[target, seqs].astype(jnp.float32) + arrived.astype(jnp.float32)
        ).astype(jnp.bfloat16)

    def head_sum(k):
        if k == 0:
            gather_arrival(partner).wait_recv()
            loads[5].wait()
        else:
            gather_arrival(other_chip(k) * 2 + core).wait_recv()
            forward_copy(k).start()
            gather_arrival(other_chip(k) * 2 + 1 - core).wait_recv()
        head_sums[...] = lax.dot_general(
            contexts[seq_rows(other_chip(k) * 2, 2), :],
            out_all[...],
            TRANSPOSED,
            preferred_element_type=jnp.float32,
        )
        for target in range(depth):
            for c in range(2):
                first = c * row_count + target * part_rows
                line_send[target, other_chip(k) * 2 + c] = head_sums[
                    first : first + part_rows, :
                ].astype(jnp.bfloat16)

    def line_steps(k):
        for t in range(depth - 1):
            right_target = depth - 1 - t
            left_target = t

            @pl.when(expert < right_target)
            def _():
                @pl.when(expert > 0)
                def _():
                    line_add(k, right_target, True)

                line_copy(k, right_target, True).start()

            @pl.when(expert > left_target)
            def _():
                @pl.when(expert < depth - 1)
                def _():
                    line_add(k, left_target, False)

                line_copy(k, left_target, False).start()

    def seq_copy(seq):
        return send(
            seq_send.at[seq],
            seq_recv.at[me],
            seq_send_sem.at[seq],
            seq_recv_sem.at[me],
            {"attn": seq},
        )

    def seq_arrival(seq):
        return send(
            seq_send.at[seq],
            seq_recv.at[seq],
            seq_send_sem.at[seq],
            seq_recv_sem.at[seq],
            {"attn": seq},
        )

    def line_end(k):
        seqs = pl.ds(other_chip(k) * 2, 2)

        @pl.when(expert > 0)
        def _():
            line_add(k, expert, True)

        @pl.when(expert < depth - 1)
        def _():
            line_add(k, expert, False)

        seq_send[seqs] = line_send[expert, seqs]
        if k == 0:
            seq_copy(partner).start()
            seq_recv[me] = seq_send[me]
        else:
            seq_copy(other_chip(k) * 2 + core).start()
            seq_copy(other_chip(k) * 2 + 1 - core).start()

    for k in range(chips):
        head_sum(k)
        line_steps(k)
    for k in range(chips):
        line_end(k)

    for k in range(1, n):
        seq_arrival(lax.rem(me + k, n)).wait_recv()
    my_rows = pl.ds(pl.multiple_of(expert * part_rows, part_rows), part_rows)
    for f in range(n):
        columns = slice(f * block, (f + 1) * block)
        states[expert, :, columns] = (
            tokens_ref[my_rows, columns].astype(jnp.float32) + seq_recv[f].astype(jnp.float32)
        ).astype(jnp.bfloat16)

    def state_copy(index, rightward):
        return send(
            states.at[index],
            states.at[index],
            (state_right if rightward else state_left).at[index],
            state_recv.at[index],
            {"expert": lax.rem(expert + (1 if rightward else depth - 1), depth)},
        )

    def spread(index, rightward):
        @pl.when((expert < depth - 1) if rightward else (expert > 0))
        def _():
            state_copy(index, rightward).start()

    def take(index):
        state_ref[index] = states[index]
        for i in range(0, part_rows, 16):
            rows = pl.ds(pl.multiple_of(index * part_rows + i, 16), 16)
            post[rows, :] = norm(
                states[index, i : i + 16, :].astype(jnp.float32), post_gain_ref[...]
            )

    spread(expert, True)
    spread(expert, False)
    take(expert)
    for t in range(1, depth):

        @pl.when(expert >= t)
        def _():
            state_copy(expert - t, True).wait_recv()
            spread(expert - t, True)

        @pl.when(expert + t < depth)
        def _():
            state_copy(expert + t, False).wait_recv()
            spread(expert + t, False)

        @pl.when(expert >= t)
        def _():
            take(expert - t)

        @pl.when(expert + t < depth)
        def _():
            take(expert + t)

    for start in range(0, model_width, 1024):
        columns = slice(start, start + 1024)
        buffer_ref[:, columns] = jnp.dot(
            dispatch_ref[...], post[:, columns], preferred_element_type=jnp.float32
        ).astype(jnp.bfloat16)

    for k in range(1, n):
        piece_copy(lax.rem(me + k, n)).wait_send()
        seq_copy(lax.rem(me + k, n)).wait_send()
    for k in range(chips):
        pair_copy(k).wait_send()
        gather_copy(k).wait_send()
        if k > 0:
            chip_copy(k).wait_send()
            forward_copy(k).wait_send()
        for target in range(depth):

            @pl.when(expert < target)
            def _():
                line_copy(k, target, True).wait_send()

            @pl.when(expert > target)
            def _():
                line_copy(k, target, False).wait_send()

    for index in range(depth):

        @pl.when((expert < depth - 1) & (index <= expert))
        def _():
            state_copy(index, True).wait_send()

        @pl.when((expert > 0) & (index >= expert))
        def _():
            state_copy(index, False).wait_send()


def attention_layer(
    tokens,
    norm_gain,
    cosine,
    sine,
    bias,
    post_gain,
    dispatch,
    query_weight,
    key_weight,
    value_weight,
    listed_keys,
    listed_values,
    out_weight,
):
    n = lax.axis_size("attn")
    depth = lax.axis_size("expert")
    chips = n // 2
    row_count, model_width = tokens.shape
    block = model_width // n
    query_columns = query_weight.shape[1]
    key_columns = key_weight.shape[1]
    projected = query_columns + 2 * key_columns
    part_rows = row_count // depth
    out_features = out_weight.shape[0]
    group_rows = query_columns // key_columns * row_count
    vmem = pl.BlockSpec(memory_space=pltpu.VMEM)
    anywhere = pl.BlockSpec(memory_space=pl.ANY)
    dma = pltpu.SemaphoreType.DMA
    bf16 = jnp.bfloat16
    buffer, state = pl.pallas_call(
        functools.partial(attention_kernel, chips, depth),
        out_shape=(
            jax.ShapeDtypeStruct((dispatch.shape[0], model_width), bf16),
            jax.ShapeDtypeStruct((depth, part_rows, model_width), bf16),
        ),
        in_specs=[vmem] * 7 + [anywhere] * 6,
        out_specs=(vmem, vmem),
        scratch_shapes=[
            pltpu.VMEM(query_weight.shape, bf16),
            pltpu.VMEM(key_weight.shape, bf16),
            pltpu.VMEM(value_weight.shape, bf16),
            pltpu.VMEM(listed_keys.shape, bf16),
            pltpu.VMEM(listed_values.shape, bf16),
            pltpu.VMEM(out_weight.shape, bf16),
            pltpu.VMEM((n, row_count, block), bf16),
            pltpu.VMEM((n * row_count, block), bf16),
            pltpu.VMEM((2 * row_count, projected), jnp.float32),
            pltpu.VMEM((chips, row_count, projected), jnp.float32),
            pltpu.VMEM((chips, row_count, projected), bf16),
            pltpu.VMEM((chips, row_count, projected), bf16),
            pltpu.VMEM((chips, row_count, projected), bf16),
            pltpu.VMEM((chips, row_count, projected), bf16),
            pltpu.VMEM((row_count, projected), jnp.float32),
            pltpu.VMEM((bias.shape[0] + 1, group_rows, row_count), jnp.float32),
            pltpu.VMEM((n * row_count, query_columns), bf16),
            pltpu.VMEM((2 * row_count, out_features), jnp.float32),
            pltpu.VMEM((depth, n, part_rows, out_features), bf16),
            pltpu.VMEM((depth, n, part_rows, out_features), bf16),
            pltpu.VMEM((depth, n, part_rows, out_features), bf16),
            pltpu.VMEM((n, part_rows, out_features), bf16),
            pltpu.VMEM((n, part_rows, out_features), bf16),
            pltpu.VMEM((depth, part_rows, model_width), bf16),
            pltpu.VMEM((row_count, model_width), bf16),
            dma((6,)),
            dma((n,)),
            dma((n,)),
            dma((chips,)),
            dma((chips,)),
            dma((chips,)),
            dma((chips,)),
            dma((chips,)),
            dma((chips,)),
            dma((n,)),
            dma((depth, chips)),
            dma((depth, chips)),
            dma((depth, chips)),
            dma((n,)),
            dma((n,)),
            dma((depth,)),
            dma((depth,)),
            dma((depth,)),
        ],
        compiler_params=pltpu.CompilerParams(
            collective_id=1, has_side_effects=True, vmem_limit_bytes=56 * 1024 * 1024
        ),
    )(
        tokens,
        norm_gain[None, :],
        cosine,
        sine,
        bias,
        post_gain[None, :],
        dispatch,
        query_weight,
        key_weight,
        value_weight,
        listed_keys,
        listed_values,
        out_weight,
    )
    return buffer, state.reshape(row_count, model_width)


def shards(
    tokens,
    norm_gain,
    query_weight,
    key_weight,
    value_weight,
    out_weight,
    cache_key,
    cache_value,
    block_table,
    block_count,
    expert_ids,
    gate_weights,
    post_gain,
    expert_gate,
    expert_up,
    expert_down,
):
    expert_axis_size = lax.axis_size("expert")
    expert_index = lax.axis_index("expert")
    row_count = tokens.shape[0]
    model_width = tokens.shape[1]
    share_width = model_width // expert_axis_size
    expert_total = expert_axis_size * expert_gate.shape[0]
    capacity = 3 * row_count // expert_total
    row_range = jnp.arange(row_count, dtype=jnp.int32)
    positions = (block_count[0] * BLK + row_range).astype(jnp.float32)
    half = HD // 2
    frequency = jnp.exp(
        jnp.arange(half, dtype=jnp.float32) * (-2.0 * math.log(rope_base) / HD)
    )
    angles = positions[:, None] * frequency[None, :]
    cosine = jnp.cos(angles)
    sine_part = jnp.sin(angles)
    slots = pair_slots(expert_ids, expert_total)
    slot_range = jnp.arange(capacity, dtype=jnp.int32)
    picks = [
        (expert_ids[:, pick] == expert_index)[:, None]
        & (slot_range[None, :] == slots[:, pick][:, None])
        for pick in range(2)
    ]
    listed_keys, listed_values = listed_blocks(block_table, cache_key, cache_value)
    live = jnp.arange(block_table.shape[1], dtype=jnp.int32) < block_count[0]
    bias = jnp.broadcast_to(
        jnp.where(live, 0.0, -jnp.inf).astype(jnp.float32)[:, None], (live.shape[0], BLK)
    )
    buffer, state = attention_layer(
        tokens,
        norm_gain,
        jnp.concatenate([cosine, cosine], axis=1),
        jnp.concatenate([-sine_part, sine_part], axis=1),
        bias,
        post_gain,
        (picks[0] | picks[1]).T.astype(jnp.bfloat16),
        query_weight,
        key_weight,
        value_weight,
        listed_keys,
        listed_values,
        out_weight,
    )
    state_share = lax.dynamic_slice_in_dim(state, expert_index * share_width, share_width, 1)
    mixture = expert_layer(
        buffer,
        expert_gate,
        expert_up,
        expert_down,
        jnp.stack(picks).astype(jnp.bfloat16),
        gate_weights,
    )
    return (state_share.astype(jnp.float32) + mixture).astype(jnp.bfloat16)


def solution(mesh):
    return jax.shard_map(
        shards,
        mesh=mesh,
        in_specs=(
            P(("groups", "attn"), None),
            P(),
            P("attn", "expert"),
            P("attn", "expert"),
            P("attn", "expert"),
            P("attn", "expert"),
            P(("groups", "attn"), None, "expert"),
            P(("groups", "attn"), None, "expert"),
            P(("groups", "attn"), None),
            P(("groups", "attn")),
            P(("groups", "attn"), None),
            P(("groups", "attn"), None),
            P(),
            P("expert", None, "attn"),
            P("expert", None, "attn"),
            P("expert", "attn", None),
        ),
        out_specs=P(("groups", "attn"), "expert"),
        check_vma=False,
    )
```

time: 386 us -> 175 us (0.45)
  waiting for transfers between devices: 235 us -> 0 us
  Pallas kernels: 0 us -> 160 us
  matrix products: 54.4 us -> 0 us
  blocking collectives: 46.9 us -> 0 us
  between operations: 14.5 us -> 0.78 us
  local copies, waits for them, and re-layouts: 18.6 us -> 6.94 us
  other arithmetic: 15.6 us -> 4.66 us
    pallas_call x0 -> x3, Pallas kernels: none -> 160 us  [the longest x1 94.5 us: attention_layer(): pl.pallas_call(functools.partial(attention_kernel, chips, depth), out_sha...]
    reduce_scatter x3 -> x0, waiting for transfers between devices: 107 us -> none  [the longest x1 44 us: shards(): lax.psum_scatter(first_term + second_term, 'expert', scatter_dimension=1,...]
    psum x1 -> x0, waiting for transfers between devices: 84.2 us -> none  [shards(): attended = lax.psum(by_rows, 'expert')]
    dot_general x11 -> x0, matrix products: 54.4 us -> none  [the longest x1 24.7 us: shards(): jnp.dot(activated, down_local, preferred_element_type=jnp.float32)]
    all_to_all x2 -> x0, blocking collectives: 46.9 us -> none  [the longest x1 28.2 us: shards(): lax.all_to_all(partial_heads, 'attn', split_axis=0, concat_axis=1, tiled=...]
    all_gather x2 -> x0, waiting for transfers between devices: 44.5 us -> none  [the longest x1 27.6 us: shards(): piece = lax.all_gather(buffer, 'attn', axis=0, tiled=True)]
    reduce_sum x6 -> x0, other arithmetic: 6.65 us -> none  [the longest x2 3.54 us: layer_norm(): center = jnp.mean(values, axis=-1, keepdims=True)]
    gather x2 -> x0, local copies, waits for them, and re-layouts: 5.22 us -> none  [the longest x1 2.61 us: shards(): jnp.take(cache_key[0].reshape(CACHE_BLOCKS, BLK, key_columns), block_tabl...]
  transfers between devices with their start and end apart: 6 -> 0, of which waited for: 6 -> 0; matrix products, arithmetic and copies ran while one was open for 4% -> 0% of each run, Pallas kernels for 0% -> 0%
where the time goes in v1:
time: 175 us; the launch traced here: 172 us
  Pallas kernels  160 us (91%)
  local copies, waits for them, and re-layouts  6.94 us (4%)
  other arithmetic  4.66 us (3%)
    pallas_call x1, Pallas kernels, attention_layer(): pl.pallas_call(functools.partial(attention_kernel, chips, depth), out_sha...  94.5 us
    pallas_call x1, Pallas kernels, expert_layer(): pl.pallas_call(functools.partial(moe_kernel, chips, depth), out_shape=jax...  62.4 us

profile of v1, /device:TPU:0, one launch (start us, length us, event | category | flops | bytes accessed | tf_op | source)
XLA Modules:
  0.0 172.3 jit_solution(8612804192873088087)
XLA Ops:
  0.0 0.8 copy.28
  0.8 0.1 eq.102
  0.9 1.2 reduce-window.6
  2.2 0.1 slice.24
  2.2 0.1 copy.30
  2.4 0.1 copy.31
  2.5 0.1 add_bitcast_fusion
  2.6 0.1 eq.98
  2.7 0.1 reshape.180
  2.9 0.2 slice_reduce_fusion.1
  3.1 0.8 compare_bitcast_fusion.1
  3.8 0.6 fusion.5.dispatch_ref
  5.1 0.3 fusion.7
  5.4 0.7 pad_maximum_fusion
  6.2 3.0 %shard_map.154 = (bf16[1024,256]{1,0:T(8,128)(2,1)}, bf16[1024,256]{1,0:T(8,128)(2,1)}) custom-call(s32[1,8]{1,0:T(1,128)} %table_ref.1, bf16[1,2048,256]{2,1,0:T(8,128)(2,1)} %cache_key_ref.1, bf16[1,2048,256]{2,1,0:T(8,128)(2,1)} %cache_value_ref.1), custom_call_target="tpu_custom_call" | custom-call | tf_op jit(solution)/shard_map/pallas_call | solution.py:396
  9.2 0.7 broadcast_in_dim.30.bias_ref
  9.9 94.5 %shard_map.155 = (bf16[96,4096]{1,0:T(8,128)(2,1)}, bf16[4,32,4096]{2,1,0:T(8,128)(2,1)}) custom-call(bf16[128,4096]{1,0:T(8,128)(2,1)} %tokens_ref.1, f32[1,4096]{1,0:T(1,128)} %bitcast.38, f32[128,128]{1,0:T(8,128)} %get-tuple-element.20.cosine_ref, f32[128,128]{1,0:T(8,128)} %get-tuple-element.21.sine_ref, f32[8,128]{1,0:T(8,128)} %broadcast_in_dim.30.bias_ref, ...), custom_call_target="tpu_custom_call" | custom-call | tf_op jit(solution)/shard_map/pallas_call | solution.py:935
  104.4 0.1 fusion.1
  104.5 0.7 add_convert_fusion.picks_ref
  105.2 1.4 copy.33.weights_ref
  106.6 62.4 %shard_map.156 = f32[2,128,512]{2,1,0:T(8,128)} custom-call(bf16[96,4096]{1,0:T(8,128)(2,1)} %get-tuple-element.12.buffer_ref, bf16[1,1600,4096]{2,1,0:T(8,128)(2,1)} %bitcast.41, bf16[1,1600,4096]{2,1,0:T(8,128)(2,1)} %bitcast.42, bf16[1,1600,4096]{2,1,0:T(8,128)(2,1)} %down_ref.1, bf16[2,128,96]{2,1,0:T(8,128)(2,1)} %add_convert_fusion.picks_ref, ...), custom_call_target="tpu_custom_call" | custom-call | flops 15099494400 | bytes 39321600 | tf_op jit(solution)/shard_map/pallas_call | solution.py:331
  169.0 1.2 copy.34
  170.3 1.0 constant_dynamic-slice_fusion
  171.2 0.2 copy.36
  171.4 0.1 fusion
  171.5 0.9 copy.35
  (7 shorter events, 0.1 us)

commit v2 on v1

--- a/solution.py
+++ b/solution.py
@@ -18,15 +18,6 @@
 
 epsilon = 1e-05
 rope_base = 10000.0
-
-
-def pair_slots(expert_ids, expert_total):
-    flat_ids = expert_ids.reshape(-1)
-    onehot = (flat_ids[:, None] == jnp.arange(expert_total, dtype=jnp.int32)[None, :]).astype(
-        jnp.int32
-    )
-    earlier = jnp.cumsum(onehot, axis=0) - onehot
-    return jnp.sum(onehot * earlier, axis=1).reshape(expert_ids.shape)
 
 
 def moe_kernel(
@@ -36,8 +27,8 @@
     gate_ref,
     up_ref,
     down_ref,
-    picks_ref,
-    weights_ref,
+    combine_ref,
+    share_ref,
     out_ref,
     gate_all,
     up_all,
@@ -51,6 +42,7 @@
     chip_send,
     chip_recv,
     mine,
+    own_mix,
     mix_send,
     mix_recv,
     load_sem,
@@ -256,10 +248,11 @@
             chip_arrival(step, k).wait_recv()
             total = total + chip_recv[step, other_chip(k)].astype(jnp.float32)
         expert_out = total.astype(jnp.bfloat16)
-        mixture = weights_ref[:, 0:1] * jnp.dot(
-            picks_ref[0], expert_out, preferred_element_type=jnp.float32
-        ) + weights_ref[:, 1:2] * jnp.dot(
-            picks_ref[1], expert_out, preferred_element_type=jnp.float32
+        mixture = lax.dot_general(
+            combine_ref[...],
+            expert_out,
+            (((0,), (0,)), ((), ())),
+            preferred_element_type=jnp.float32,
         )
         part = lax.rem(step, per_owner)
 
@@ -270,7 +263,7 @@
 
         @pl.when(step >= steps - per_owner)
         def _():
-            out_ref[part] = mixture
+            own_mix[part] = mixture
 
     def step_body(step, carry):
         @pl.when(step < steps)
@@ -290,11 +283,12 @@
     lax.fori_loop(0, steps + LAG, step_body, 0)
 
     for part in range(per_owner):
-        total = out_ref[part]
+        columns = slice(part * width, (part + 1) * width)
+        total = share_ref[:, columns].astype(jnp.float32) + own_mix[part]
         for k in range(1, depth):
             mix_arrival(other_expert(k), part).wait_recv()
             total = total + mix_recv[other_expert(k), part].astype(jnp.float32)
-        out_ref[part] = total
+        out_ref[:, columns] = total.astype(jnp.bfloat16)
 
     for k in range(chips):
         gather_copy(k).wait_send()
@@ -314,13 +308,13 @@
     lax.fori_loop(0, steps, finish, 0)
 
 
-def expert_layer(buffer, gate, up, down, picks, weights):
+def expert_layer(buffer, gate, up, down, combine, share_state):
     n = lax.axis_size("attn")
     depth = lax.axis_size("expert")
     chips = n // 2
     capacity, model_width = buffer.shape
     hidden = gate.shape[2]
-    row_count = weights.shape[0]
+    row_count = share_state.shape[0]
     share = model_width // depth
     width = math.gcd(share, 512)
     per_owner = share // width
@@ -328,9 +322,9 @@
     vmem = pl.BlockSpec(memory_space=pltpu.VMEM)
     anywhere = pl.BlockSpec(memory_space=pl.ANY)
     dma = pltpu.SemaphoreType.DMA
-    out = pl.pallas_call(
+    return pl.pallas_call(
         functools.partial(moe_kernel, chips, depth),
-        out_shape=jax.ShapeDtypeStruct((per_owner, row_count, width), jnp.float32),
+        out_shape=jax.ShapeDtypeStruct((row_count, share), jnp.bfloat16),
         in_specs=[vmem, anywhere, anywhere, anywhere, vmem, vmem],
         out_specs=vmem,
         scratch_shapes=[
@@ -346,6 +340,7 @@
             pltpu.VMEM((steps, chips, capacity, width), jnp.bfloat16),
             pltpu.VMEM((steps, chips, capacity, width), jnp.bfloat16),
             pltpu.VMEM((steps, capacity, width), jnp.float32),
+            pltpu.VMEM((per_owner, row_count, width), jnp.float32),
             pltpu.VMEM((steps, row_count, width), jnp.bfloat16),
             pltpu.VMEM((depth, per_owner, row_count, width), jnp.bfloat16),
             dma((3,)),
@@ -367,8 +362,7 @@
             bytes_accessed=6 * model_width * hidden,
             transcendentals=n * capacity * hidden,
         ),
-    )(buffer, gate.swapaxes(1, 2), up.swapaxes(1, 2), down, picks, weights)
-    return out.transpose(1, 0, 2).reshape(row_count, share)
+    )(buffer, gate.swapaxes(1, 2), up.swapaxes(1, 2), down, combine, share_state)
 
 
 def listed_kernel(table_ref, cache_key_ref, cache_value_ref, keys_ref, values_ref, sems):
@@ -411,7 +405,8 @@
     sine_ref,
     bias_ref,
     post_gain_ref,
-    dispatch_ref,
+    ids_ref,
+    gates_ref,
     query_weight_ref,
     key_weight_ref,
     value_weight_ref,
@@ -419,13 +414,15 @@
     cache_value_ref,
     out_weight_ref,
     buffer_ref,
-    state_ref,
+    combine_ref,
+    share_ref,
     query_all,
     key_all,
     value_all,
     cache_keys,
     cache_values,
     out_all,
+    turns,
     normed,
     pieces,
     partial,
@@ -475,6 +472,8 @@
     query_columns = query_all.shape[1]
     key_columns = key_all.shape[1]
     part_rows = row_count // depth
+    halves = line_send.shape[1]
+    half_rows = row_count // 2
     loads = [
         pltpu.make_async_copy(source, target, load_sem.at[i])
         for i, (source, target) in enumerate(
@@ -526,93 +525,106 @@
         rows = pl.ds(pl.multiple_of(i * 16, 16), 16)
         result = norm(tokens_ref[rows, :].astype(jnp.float32), gain_ref[...])
         for f in range(n):
-            normed[f, rows, :] = result[:, f * block : (f + 1) * block]
+            normed[f, i // per_half, pl.ds(pl.multiple_of(i % per_half * 16, 16), 16), :] = result[
+                :, f * block : (f + 1) * block
+            ]
         return carry
+
+    per_half = half_rows // 16
 
     lax.fori_loop(0, row_count // 16, norm_rows, 0)
     pl.semaphore_wait(barrier, n - 1 + depth - 1)
 
-    def piece_copy(seq):
-        return send(
-            normed.at[seq],
-            pieces.at[seq_rows(me)],
-            piece_send.at[seq],
-            piece_recv.at[me],
+    def half_seq(seq, count=1):
+        return pl.ds(pl.multiple_of(seq * half_rows, half_rows), count * half_rows)
+
+    def piece_copy(seq, h):
+        return send(
+            normed.at[seq, h],
+            pieces.at[h, half_seq(me)],
+            piece_send.at[seq, h],
+            piece_recv.at[me, h],
             {"attn": seq},
         )
 
-    def piece_arrival(seq):
-        return send(
-            normed.at[seq],
-            pieces.at[seq_rows(seq)],
-            piece_send.at[seq],
-            piece_recv.at[seq],
+    def piece_arrival(seq, h):
+        return send(
+            normed.at[seq, h],
+            pieces.at[h, half_seq(seq)],
+            piece_send.at[seq, h],
+            piece_recv.at[seq, h],
             {"attn": seq},
         )
 
-    for k in range(1, chips):
-        piece_copy(other_chip(k) * 2 + core).start()
-        piece_copy(other_chip(k) * 2 + 1 - core).start()
-    piece_copy(partner).start()
-    pieces[seq_rows(me), :] = normed[me]
-
-    def pair_copy(k):
-        return send(
-            pair_send.at[k],
-            pair_recv.at[k],
-            pair_send_sem.at[k],
-            pair_recv_sem.at[k],
+    for h in range(2):
+        for k in range(1, chips):
+            piece_copy(other_chip(k) * 2 + core, h).start()
+            piece_copy(other_chip(k) * 2 + 1 - core, h).start()
+        piece_copy(partner, h).start()
+        pieces[h, half_seq(me), :] = normed[me, h]
+
+    def pair_copy(k, h):
+        return send(
+            pair_send.at[k, h],
+            pair_recv.at[k, h],
+            pair_send_sem.at[k, h],
+            pair_recv_sem.at[k, h],
             {"attn": partner},
         )
 
-    def chip_copy(k):
-        return send(
-            chip_send.at[k],
-            chip_recv.at[chip],
-            chip_send_sem.at[k],
-            chip_recv_sem.at[chip],
+    def chip_copy(k, h):
+        return send(
+            chip_send.at[k, h],
+            chip_recv.at[chip, h],
+            chip_send_sem.at[k, h],
+            chip_recv_sem.at[chip, h],
             {"attn": other_chip(k) * 2 + core},
         )
 
-    def chip_arrival(k):
-        return send(
-            chip_send.at[k],
-            chip_recv.at[other_chip(k)],
-            chip_send_sem.at[k],
-            chip_recv_sem.at[other_chip(k)],
+    def chip_arrival(k, h):
+        return send(
+            chip_send.at[k, h],
+            chip_recv.at[other_chip(k), h],
+            chip_send_sem.at[k, h],
+            chip_recv_sem.at[other_chip(k), h],
             {"attn": other_chip(k) * 2 + core},
         )
 
+    turns[0] = jnp.concatenate([cosine_ref[...], cosine_ref[...]], axis=1)
+    turns[1] = jnp.concatenate([-sine_ref[...], sine_ref[...]], axis=1)
+    for load in loads[:3]:
+        load.wait()
     for k in range(chips):
-        if k == 0:
-            for load in loads[:3]:
-                load.wait()
-        else:
-            piece_arrival(other_chip(k) * 2 + core).wait_recv()
-        if k == 0:
-            piece_arrival(partner).wait_recv()
-        else:
-            piece_arrival(other_chip(k) * 2 + 1 - core).wait_recv()
-        rows = pieces[seq_rows(other_chip(k) * 2, 2), :]
-        start = 0
-        for weight in (query_all, key_all, value_all):
-            size = weight.shape[1]
-            partial[:, start : start + size] = jnp.dot(
-                rows, weight[...], preferred_element_type=jnp.float32
-            )
-            start += size
-        keep[k] = partial[seq_rows(core), :]
-        pair_send[k] = partial[seq_rows(1 - core), :].astype(jnp.bfloat16)
-        pair_copy(k).start()
-        if k > 0:
-            pair_copy(k).wait_recv()
-            chip_send[k] = (keep[k] + pair_recv[k].astype(jnp.float32)).astype(jnp.bfloat16)
-            chip_copy(k).start()
-    pair_copy(0).wait_recv()
-    projected[...] = keep[0] + pair_recv[0].astype(jnp.float32)
-    for k in range(1, chips):
-        chip_arrival(k).wait_recv()
-        projected[...] = projected[...] + chip_recv[other_chip(k)].astype(jnp.float32)
+        for h in range(2):
+            if k > 0:
+                piece_arrival(other_chip(k) * 2 + core, h).wait_recv()
+                piece_arrival(other_chip(k) * 2 + 1 - core, h).wait_recv()
+            else:
+                piece_arrival(partner, h).wait_recv()
+            rows = pieces[h, half_seq(other_chip(k) * 2, 2), :]
+            start = 0
+            for weight in (query_all, key_all, value_all):
+                size = weight.shape[1]
+                partial[:, start : start + size] = jnp.dot(
+                    rows, weight[...], preferred_element_type=jnp.float32
+                )
+                start += size
+            keep[k, h] = partial[half_seq(core), :]
+            pair_send[k, h] = partial[half_seq(1 - core), :].astype(jnp.bfloat16)
+            pair_copy(k, h).start()
+            if k > 0:
+                pair_copy(k, h).wait_recv()
+                chip_send[k, h] = (keep[k, h] + pair_recv[k, h].astype(jnp.float32)).astype(
+                    jnp.bfloat16
+                )
+                chip_copy(k, h).start()
+    for h in range(2):
+        pair_copy(0, h).wait_recv()
+        total = keep[0, h] + pair_recv[0, h].astype(jnp.float32)
+        for k in range(1, chips):
+            chip_arrival(k, h).wait_recv()
+            total = total + chip_recv[other_chip(k), h].astype(jnp.float32)
+        projected[h * half_rows : (h + 1) * half_rows, :] = total
 
     loads[3].wait()
     loads[4].wait()
@@ -622,7 +634,42 @@
     def turned(start):
         values = projected[:, start : start + HD]
         swapped = jnp.concatenate([values[:, half:], values[:, :half]], axis=1)
-        return (values * cosine_ref[...] + swapped * sine_ref[...]).astype(jnp.bfloat16)
+        return (values * turns[0] + swapped * turns[1]).astype(jnp.bfloat16)
+
+    key_heads = key_columns // HD
+
+    def head_part(seq, head):
+        width = group * HD
+        return contexts.at[seq_rows(seq), pl.ds(head * width, width)]
+
+    def gather_copy(k, head):
+        where = {"attn": partner} if k == 0 else {"attn": other_chip(k) * 2 + core}
+        return send(
+            head_part(me, head),
+            head_part(me, head),
+            gather_send.at[k, head],
+            gather_recv.at[me, head],
+            where,
+        )
+
+    def forward_copy(k, head):
+        seq = other_chip(k) * 2 + core
+        return send(
+            head_part(seq, head),
+            head_part(seq, head),
+            forward_send.at[k, head],
+            gather_recv.at[seq, head],
+            {"attn": partner},
+        )
+
+    def gather_arrival(seq, head):
+        return send(
+            head_part(seq, head),
+            head_part(seq, head),
+            gather_send.at[0, head],
+            gather_recv.at[seq, head],
+            {"attn": partner},
+        )
 
     score_scale = 1.0 / math.sqrt(HD)
     listed = bias_ref.shape[0]
@@ -661,12 +708,12 @@
             exponent = jnp.exp(scores[j] - largest)
             scores[j] = exponent
             total = total + exponent
-        denominator = jnp.sum(total, axis=-1, keepdims=True)
+        inverse = 1.0 / jnp.sum(total, axis=-1, keepdims=True)
         context = jnp.zeros((group_rows, HD), jnp.float32)
         for j in range(listed + 1):
             values = fresh_values if j == listed else cache_values[cache_rows(j), columns]
             context = context + jnp.dot(
-                (scores[j] / denominator).astype(jnp.bfloat16),
+                (scores[j] * inverse).astype(jnp.bfloat16),
                 values,
                 preferred_element_type=jnp.float32,
             )
@@ -675,66 +722,42 @@
             contexts[seq_rows(me), start : start + HD] = context[
                 g * row_count : (g + 1) * row_count
             ].astype(jnp.bfloat16)
-
-    def gather_copy(k):
-        where = {"attn": partner} if k == 0 else {"attn": other_chip(k) * 2 + core}
-        return send(
-            contexts.at[seq_rows(me)],
-            contexts.at[seq_rows(me)],
-            gather_send.at[k],
-            gather_recv.at[me],
-            where,
-        )
-
-    def forward_copy(k):
-        seq = other_chip(k) * 2 + core
-        return send(
-            contexts.at[seq_rows(seq)],
-            contexts.at[seq_rows(seq)],
-            forward_send.at[k],
-            gather_recv.at[seq],
-            {"attn": partner},
-        )
-
-    def gather_arrival(seq):
-        return send(
-            contexts.at[seq_rows(seq)],
-            contexts.at[seq_rows(seq)],
-            gather_send.at[0],
-            gather_recv.at[seq],
-            {"attn": partner},
-        )
-
-    for k in range(1, chips):
-        gather_copy(k).start()
-    gather_copy(0).start()
-
-    def line_copy(k, target, rightward):
+        for k in range(1, chips):
+            gather_copy(k, head).start()
+        gather_copy(0, head).start()
+
+    def line_copy(k, h, target, rightward):
         seqs = pl.ds(other_chip(k) * 2, 2)
         return send(
-            line_send.at[target, seqs],
-            (from_left if rightward else from_right).at[target, seqs],
-            line_send_sem.at[target, k],
-            (left_sem if rightward else right_sem).at[target, k],
+            line_send.at[target, h, seqs],
+            (from_left if rightward else from_right).at[target, h, seqs],
+            line_send_sem.at[target, k, h],
+            (left_sem if rightward else right_sem).at[target, k, h],
             {"expert": lax.rem(expert + (1 if rightward else depth - 1), depth)},
         )
 
-    def line_add(k, target, rightward):
+    def line_add(k, h, target, rightward):
         seqs = pl.ds(other_chip(k) * 2, 2)
-        line_copy(k, target, rightward).wait_recv()
-        arrived = (from_left if rightward else from_right)[target, seqs]
-        line_send[target, seqs] = (
-            line_send[target, seqs].astype(jnp.float32) + arrived.astype(jnp.float32)
+        line_copy(k, h, target, rightward).wait_recv()
+        arrived = (from_left if rightward else from_right)[target, h, seqs]
+        line_send[target, h, seqs] = (
+            line_send[target, h, seqs].astype(jnp.float32) + arrived.astype(jnp.float32)
         ).astype(jnp.bfloat16)
 
+    step_rows = part_rows // halves
+
     def head_sum(k):
+        for head in range(key_heads):
+            if k == 0:
+                gather_arrival(partner, head).wait_recv()
+            else:
+                gather_arrival(other_chip(k) * 2 + core, head).wait_recv()
+                forward_copy(k, head).start()
         if k == 0:
-            gather_arrival(partner).wait_recv()
             loads[5].wait()
         else:
-            gather_arrival(other_chip(k) * 2 + core).wait_recv()
-            forward_copy(k).start()
-            gather_arrival(other_chip(k) * 2 + 1 - core).wait_recv()
+            for head in range(key_heads):
+                gather_arrival(other_chip(k) * 2 + 1 - core, head).wait_recv()
         head_sums[...] = lax.dot_general(
             contexts[seq_rows(other_chip(k) * 2, 2), :],
             out_all[...],
@@ -742,13 +765,14 @@
             preferred_element_type=jnp.float32,
         )
         for target in range(depth):
-            for c in range(2):
-                first = c * row_count + target * part_rows
-                line_send[target, other_chip(k) * 2 + c] = head_sums[
-                    first : first + part_rows, :
-                ].astype(jnp.bfloat16)
-
-    def line_steps(k):
+            for h in range(halves):
+                for c in range(2):
+                    first = c * row_count + target * part_rows + h * step_rows
+                    line_send[target, h, other_chip(k) * 2 + c] = head_sums[
+                        first : first + step_rows, :
+                    ].astype(jnp.bfloat16)
+
+    def line_steps(k, h):
         for t in range(depth - 1):
             right_target = depth - 1 - t
             left_target = t
@@ -757,149 +781,203 @@
             def _():
                 @pl.when(expert > 0)
                 def _():
-                    line_add(k, right_target, True)
-
-                line_copy(k, right_target, True).start()
+                    line_add(k, h, right_target, True)
+
+                line_copy(k, h, right_target, True).start()
 
             @pl.when(expert > left_target)
             def _():
                 @pl.when(expert < depth - 1)
                 def _():
-                    line_add(k, left_target, False)
-
-                line_copy(k, left_target, False).start()
-
-    def seq_copy(seq):
-        return send(
-            seq_send.at[seq],
-            seq_recv.at[me],
-            seq_send_sem.at[seq],
-            seq_recv_sem.at[me],
+                    line_add(k, h, left_target, False)
+
+                line_copy(k, h, left_target, False).start()
+
+    def seq_copy(seq, h):
+        return send(
+            seq_send.at[h, seq],
+            seq_recv.at[h, me],
+            seq_send_sem.at[h, seq],
+            seq_recv_sem.at[h, me],
             {"attn": seq},
         )
 
-    def seq_arrival(seq):
-        return send(
-            seq_send.at[seq],
-            seq_recv.at[seq],
-            seq_send_sem.at[seq],
-            seq_recv_sem.at[seq],
+    def seq_arrival(seq, h):
+        return send(
+            seq_send.at[h, seq],
+            seq_recv.at[h, seq],
+            seq_send_sem.at[h, seq],
+            seq_recv_sem.at[h, seq],
             {"attn": seq},
         )
 
-    def line_end(k):
+    def line_end(k, h):
         seqs = pl.ds(other_chip(k) * 2, 2)
 
         @pl.when(expert > 0)
         def _():
-            line_add(k, expert, True)
+            line_add(k, h, expert, True)
 
         @pl.when(expert < depth - 1)
         def _():
-            line_add(k, expert, False)
-
-        seq_send[seqs] = line_send[expert, seqs]
+            line_add(k, h, expert, False)
+
+        seq_send[h, seqs] = line_send[expert, h, seqs]
         if k == 0:
-            seq_copy(partner).start()
-            seq_recv[me] = seq_send[me]
+            seq_copy(partner, h).start()
+            seq_recv[h, me] = seq_send[h, me]
         else:
-            seq_copy(other_chip(k) * 2 + core).start()
-            seq_copy(other_chip(k) * 2 + 1 - core).start()
-
-    for k in range(chips):
-        head_sum(k)
-        line_steps(k)
-    for k in range(chips):
-        line_end(k)
-
-    for k in range(1, n):
-        seq_arrival(lax.rem(me + k, n)).wait_recv()
-    my_rows = pl.ds(pl.multiple_of(expert * part_rows, part_rows), part_rows)
-    for f in range(n):
-        columns = slice(f * block, (f + 1) * block)
-        states[expert, :, columns] = (
-            tokens_ref[my_rows, columns].astype(jnp.float32) + seq_recv[f].astype(jnp.float32)
-        ).astype(jnp.bfloat16)
-
-    def state_copy(index, rightward):
-        return send(
-            states.at[index],
-            states.at[index],
-            (state_right if rightward else state_left).at[index],
-            state_recv.at[index],
+            seq_copy(other_chip(k) * 2 + core, h).start()
+            seq_copy(other_chip(k) * 2 + 1 - core, h).start()
+
+    def state_copy(index, h, rightward):
+        return send(
+            states.at[index, h],
+            states.at[index, h],
+            (state_right if rightward else state_left).at[index, h],
+            state_recv.at[index, h],
             {"expert": lax.rem(expert + (1 if rightward else depth - 1), depth)},
         )
 
-    def spread(index, rightward):
+    def spread(index, h, rightward):
         @pl.when((expert < depth - 1) if rightward else (expert > 0))
         def _():
-            state_copy(index, rightward).start()
-
-    def take(index):
-        state_ref[index] = states[index]
-        for i in range(0, part_rows, 16):
-            rows = pl.ds(pl.multiple_of(index * part_rows + i, 16), 16)
+            state_copy(index, h, rightward).start()
+
+    share = model_width // depth
+    share_columns = pl.ds(pl.multiple_of(expert * share, share), share)
+
+    def take(index, h):
+        first = index * part_rows + h * step_rows
+        share_ref[pl.ds(pl.multiple_of(first, 16), step_rows), :] = states[
+            index, h, :, share_columns
+        ]
+        for i in range(0, step_rows, 16):
+            rows = pl.ds(pl.multiple_of(first + i, 16), 16)
             post[rows, :] = norm(
-                states[index, i : i + 16, :].astype(jnp.float32), post_gain_ref[...]
+                states[index, h, i : i + 16, :].astype(jnp.float32), post_gain_ref[...]
             )
 
-    spread(expert, True)
-    spread(expert, False)
-    take(expert)
-    for t in range(1, depth):
-
-        @pl.when(expert >= t)
-        def _():
-            state_copy(expert - t, True).wait_recv()
-            spread(expert - t, True)
-
-        @pl.when(expert + t < depth)
-        def _():
-            state_copy(expert + t, False).wait_recv()
-            spread(expert + t, False)
-
-        @pl.when(expert >= t)
-        def _():
-            take(expert - t)
-
-        @pl.when(expert + t < depth)
-        def _():
-            take(expert + t)
+    def make_state(h):
+        for k in range(1, n):
+            seq_arrival(lax.rem(me + k, n), h).wait_recv()
+        first = expert * part_rows + h * step_rows
+        my_rows = pl.ds(pl.multiple_of(first, 16), step_rows)
+        for f in range(n):
+            columns = slice(f * block, (f + 1) * block)
+            states[expert, h, :, columns] = (
+                tokens_ref[my_rows, columns].astype(jnp.float32)
+                + seq_recv[h, f].astype(jnp.float32)
+            ).astype(jnp.bfloat16)
+        spread(expert, h, True)
+        spread(expert, h, False)
+
+    def hops(h):
+        for t in range(1, depth):
+
+            @pl.when(expert >= t)
+            def _():
+                state_copy(expert - t, h, True).wait_recv()
+                spread(expert - t, h, True)
+
+            @pl.when(expert + t < depth)
+            def _():
+                state_copy(expert + t, h, False).wait_recv()
+                spread(expert + t, h, False)
+
+            @pl.when(expert >= t)
+            def _():
+                take(expert - t, h)
+
+            @pl.when(expert + t < depth)
+            def _():
+                take(expert + t, h)
+
+    head_sum(0)
+    line_steps(0, 0)
+    for k in range(1, chips):
+        head_sum(k)
+        line_steps(k, 0)
+    for k in range(chips):
+        line_end(k, 0)
+    for h in range(1, halves):
+        for k in range(chips):
+            line_steps(k, h)
+
+    hits = [
+        (ids_ref[pick : pick + 1, :] == expert).astype(jnp.float32) for pick in range(2)
+    ]
+    before = (
+        lax.broadcasted_iota(jnp.int32, (row_count, row_count), 0)
+        < lax.broadcasted_iota(jnp.int32, (row_count, row_count), 1)
+    ).astype(jnp.bfloat16)
+    earlier = jnp.dot(
+        jnp.broadcast_to(hits[0] + hits[1], (16, row_count)).astype(jnp.bfloat16),
+        before,
+        preferred_element_type=jnp.float32,
+    )[0:1, :]
+    slot_range = lax.broadcasted_iota(jnp.int32, (buffer_ref.shape[0], row_count), 0).astype(
+        jnp.float32
+    )
+    first_pick = jnp.where(slot_range == earlier, hits[0], 0.0)
+    second_pick = jnp.where(slot_range == earlier + hits[0], hits[1], 0.0)
+    dispatch = (first_pick + second_pick).astype(jnp.bfloat16)
+    combine_ref[...] = (
+        first_pick * gates_ref[0:1, :] + second_pick * gates_ref[1:2, :]
+    ).astype(jnp.bfloat16)
+
+    make_state(0)
+    for h in range(1, halves):
+        for k in range(chips):
+            line_end(k, h)
+    take(expert, 0)
+    hops(0)
+    for h in range(1, halves):
+        make_state(h)
+        take(expert, h)
+        hops(h)
 
     for start in range(0, model_width, 1024):
         columns = slice(start, start + 1024)
         buffer_ref[:, columns] = jnp.dot(
-            dispatch_ref[...], post[:, columns], preferred_element_type=jnp.float32
+            dispatch, post[:, columns], preferred_element_type=jnp.float32
         ).astype(jnp.bfloat16)
 
     for k in range(1, n):
-        piece_copy(lax.rem(me + k, n)).wait_send()
-        seq_copy(lax.rem(me + k, n)).wait_send()
+        for h in range(2):
+            piece_copy(lax.rem(me + k, n), h).wait_send()
+        for h in range(halves):
+            seq_copy(lax.rem(me + k, n), h).wait_send()
     for k in range(chips):
-        pair_copy(k).wait_send()
-        gather_copy(k).wait_send()
-        if k > 0:
-            chip_copy(k).wait_send()
-            forward_copy(k).wait_send()
-        for target in range(depth):
-
-            @pl.when(expert < target)
+        for head in range(key_heads):
+            gather_copy(k, head).wait_send()
+            if k > 0:
+                forward_copy(k, head).wait_send()
+        for h in range(2):
+            pair_copy(k, h).wait_send()
+            if k > 0:
+                chip_copy(k, h).wait_send()
+        for h in range(halves):
+            for target in range(depth):
+
+                @pl.when(expert < target)
+                def _():
+                    line_copy(k, h, target, True).wait_send()
+
+                @pl.when(expert > target)
+                def _():
+                    line_copy(k, h, target, False).wait_send()
+
+    for h in range(halves):
+        for index in range(depth):
+
+            @pl.when((expert < depth - 1) & (index <= expert))
             def _():
-                line_copy(k, target, True).wait_send()
-
-            @pl.when(expert > target)
+                state_copy(index, h, True).wait_send()
+
+            @pl.when((expert > 0) & (index >= expert))
             def _():
-                line_copy(k, target, False).wait_send()
-
-    for index in range(depth):
-
-        @pl.when((expert < depth - 1) & (index <= expert))
-        def _():
-            state_copy(index, True).wait_send()
-
-        @pl.when((expert > 0) & (index >= expert))
-        def _():
-            state_copy(index, False).wait_send()
+                state_copy(index, h, False).wait_send()
 
 
 def attention_layer(
@@ -909,7 +987,9 @@
     sine,
     bias,
     post_gain,
-    dispatch,
+    ids,
+    gates,
+    capacity,
     query_weight,
     key_weight,
     value_weight,
@@ -927,19 +1007,23 @@
     projected = query_columns + 2 * key_columns
     part_rows = row_count // depth
     out_features = out_weight.shape[0]
+    halves = 2 if part_rows % 32 == 0 else 1
+    step_rows = part_rows // halves
+    key_heads = key_columns // HD
     group_rows = query_columns // key_columns * row_count
     vmem = pl.BlockSpec(memory_space=pltpu.VMEM)
     anywhere = pl.BlockSpec(memory_space=pl.ANY)
     dma = pltpu.SemaphoreType.DMA
     bf16 = jnp.bfloat16
-    buffer, state = pl.pallas_call(
+    return pl.pallas_call(
         functools.partial(attention_kernel, chips, depth),
         out_shape=(
-            jax.ShapeDtypeStruct((dispatch.shape[0], model_width), bf16),
-            jax.ShapeDtypeStruct((depth, part_rows, model_width), bf16),
+            jax.ShapeDtypeStruct((capacity, model_width), bf16),
+            jax.ShapeDtypeStruct((capacity, row_count), bf16),
+            jax.ShapeDtypeStruct((row_count, model_width // depth), bf16),
         ),
-        in_specs=[vmem] * 7 + [anywhere] * 6,
-        out_specs=(vmem, vmem),
+        in_specs=[vmem] * 8 + [anywhere] * 6,
+        out_specs=(vmem, vmem, vmem),
         scratch_shapes=[
             pltpu.VMEM(query_weight.shape, bf16),
             pltpu.VMEM(key_weight.shape, bf16),
@@ -947,43 +1031,44 @@
             pltpu.VMEM(listed_keys.shape, bf16),
             pltpu.VMEM(listed_values.shape, bf16),
             pltpu.VMEM(out_weight.shape, bf16),
-            pltpu.VMEM((n, row_count, block), bf16),
-            pltpu.VMEM((n * row_count, block), bf16),
-            pltpu.VMEM((2 * row_count, projected), jnp.float32),
-            pltpu.VMEM((chips, row_count, projected), jnp.float32),
-            pltpu.VMEM((chips, row_count, projected), bf16),
-            pltpu.VMEM((chips, row_count, projected), bf16),
-            pltpu.VMEM((chips, row_count, projected), bf16),
-            pltpu.VMEM((chips, row_count, projected), bf16),
+            pltpu.VMEM((2, row_count, HD), jnp.float32),
+            pltpu.VMEM((n, 2, row_count // 2, block), bf16),
+            pltpu.VMEM((2, n * row_count // 2, block), bf16),
+            pltpu.VMEM((row_count, projected), jnp.float32),
+            pltpu.VMEM((chips, 2, row_count // 2, projected), jnp.float32),
+            pltpu.VMEM((chips, 2, row_count // 2, projected), bf16),
+            pltpu.VMEM((chips, 2, row_count // 2, projected), bf16),
+            pltpu.VMEM((chips, 2, row_count // 2, projected), bf16),
+            pltpu.VMEM((chips, 2, row_count // 2, projected), bf16),
             pltpu.VMEM((row_count, projected), jnp.float32),
             pltpu.VMEM((bias.shape[0] + 1, group_rows, row_count), jnp.float32),
             pltpu.VMEM((n * row_count, query_columns), bf16),
             pltpu.VMEM((2 * row_count, out_features), jnp.float32),
-            pltpu.VMEM((depth, n, part_rows, out_features), bf16),
-            pltpu.VMEM((depth, n, part_rows, out_features), bf16),
-            pltpu.VMEM((depth, n, part_rows, out_features), bf16),
-            pltpu.VMEM((n, part_rows, out_features), bf16),
-            pltpu.VMEM((n, part_rows, out_features), bf16),
-            pltpu.VMEM((depth, part_rows, model_width), bf16),
+            pltpu.VMEM((depth, halves, n, step_rows, out_features), bf16),
+            pltpu.VMEM((depth, halves, n, step_rows, out_features), bf16),
+            pltpu.VMEM((depth, halves, n, step_rows, out_features), bf16),
+            pltpu.VMEM((halves, n, step_rows, out_features), bf16),
+            pltpu.VMEM((halves, n, step_rows, out_features), bf16),
+            pltpu.VMEM((depth, halves, step_rows, model_width), bf16),
             pltpu.VMEM((row_count, model_width), bf16),
             dma((6,)),
-            dma((n,)),
-            dma((n,)),
-            dma((chips,)),
-            dma((chips,)),
-            dma((chips,)),
-            dma((chips,)),
-            dma((chips,)),
-            dma((chips,)),
-            dma((n,)),
-            dma((depth, chips)),
-            dma((depth, chips)),
-            dma((depth, chips)),
-            dma((n,)),
-            dma((n,)),
-            dma((depth,)),
-            dma((depth,)),
-            dma((depth,)),
+            dma((n, 2)),
+            dma((n, 2)),
+            dma((chips, 2)),
+            dma((chips, 2)),
+            dma((chips, 2)),
+            dma((chips, 2)),
+            dma((chips, key_heads)),
+            dma((chips, key_heads)),
+            dma((n, key_heads)),
+            dma((depth, chips, halves)),
+            dma((depth, chips, halves)),
+            dma((depth, chips, halves)),
+            dma((halves, n)),
+            dma((halves, n)),
+            dma((depth, halves)),
+            dma((depth, halves)),
+            dma((depth, halves)),
         ],
         compiler_params=pltpu.CompilerParams(
             collective_id=1, has_side_effects=True, vmem_limit_bytes=56 * 1024 * 1024
@@ -995,7 +1080,8 @@
         sine,
         bias,
         post_gain[None, :],
-        dispatch,
+        ids,
+        gates,
         query_weight,
         key_weight,
         value_weight,
@@ -1003,7 +1089,6 @@
         listed_values,
         out_weight,
     )
-    return buffer, state.reshape(row_count, model_width)
 
 
 def shards(
@@ -1024,42 +1109,28 @@
     expert_up,
     expert_down,
 ):
-    expert_axis_size = lax.axis_size("expert")
-    expert_index = lax.axis_index("expert")
     row_count = tokens.shape[0]
-    model_width = tokens.shape[1]
-    share_width = model_width // expert_axis_size
-    expert_total = expert_axis_size * expert_gate.shape[0]
+    expert_total = lax.axis_size("expert") * expert_gate.shape[0]
     capacity = 3 * row_count // expert_total
-    row_range = jnp.arange(row_count, dtype=jnp.int32)
-    positions = (block_count[0] * BLK + row_range).astype(jnp.float32)
+    positions = (block_count[0] * BLK + jnp.arange(row_count, dtype=jnp.int32)).astype(jnp.float32)
     half = HD // 2
     frequency = jnp.exp(
         jnp.arange(half, dtype=jnp.float32) * (-2.0 * math.log(rope_base) / HD)
     )
     angles = positions[:, None] * frequency[None, :]
-    cosine = jnp.cos(angles)
-    sine_part = jnp.sin(angles)
-    slots = pair_slots(expert_ids, expert_total)
-    slot_range = jnp.arange(capacity, dtype=jnp.int32)
-    picks = [
-        (expert_ids[:, pick] == expert_index)[:, None]
-        & (slot_range[None, :] == slots[:, pick][:, None])
-        for pick in range(2)
-    ]
     listed_keys, listed_values = listed_blocks(block_table, cache_key, cache_value)
-    live = jnp.arange(block_table.shape[1], dtype=jnp.int32) < block_count[0]
-    bias = jnp.broadcast_to(
-        jnp.where(live, 0.0, -jnp.inf).astype(jnp.float32)[:, None], (live.shape[0], BLK)
-    )
-    buffer, state = attention_layer(
+    block_index = lax.broadcasted_iota(jnp.int32, (block_table.shape[1], BLK), 0)
+    bias = jnp.where(block_index < block_count[0], 0.0, -jnp.inf).astype(jnp.float32)
+    buffer, combine, share_state = attention_layer(
         tokens,
         norm_gain,
-        jnp.concatenate([cosine, cosine], axis=1),
-        jnp.concatenate([-sine_part, sine_part], axis=1),
+        jnp.cos(angles),
+        jnp.sin(angles),
         bias,
         post_gain,
-        (picks[0] | picks[1]).T.astype(jnp.bfloat16),
+        expert_ids.T,
+        gate_weights.T,
+        capacity,
         query_weight,
         key_weight,
         value_weight,
@@ -1067,16 +1138,7 @@
         listed_values,
         out_weight,
     )
-    state_share = lax.dynamic_slice_in_dim(state, expert_index * share_width, share_width, 1)
-    mixture = expert_layer(
-        buffer,
-        expert_gate,
-        expert_up,
-        expert_down,
-        jnp.stack(picks).astype(jnp.bfloat16),
-        gate_weights,
-    )
-    return (state_share.astype(jnp.float32) + mixture).astype(jnp.bfloat16)
+    return expert_layer(buffer, expert_gate, expert_up, expert_down, combine, share_state)
 
 
 def solution(mesh):

time: 175 us -> 177 us (1.011)
  Pallas kernels: 160 us -> 170 us
  local copies, waits for them, and re-layouts: 6.94 us -> 2.33 us
  other arithmetic: 4.66 us -> 0.98 us
    pallas_call x1, Pallas kernels: 94.5 us -> 104 us  [attention_layer(): pl.pallas_call(functools.partial(attention_kernel, chips, depth), out_sha...]
where the time goes in v2:
time: 177 us; the launch traced here: 174 us
  Pallas kernels  170 us (96%)
  local copies, waits for them, and re-layouts  2.33 us (1%)
    pallas_call x1, Pallas kernels, attention_layer(): pl.pallas_call(functools.partial(attention_kernel, chips, depth), out_sha...  104 us
    pallas_call x1, Pallas kernels, expert_layer(): pl.pallas_call(functools.partial(moe_kernel, chips, depth), out_shape=jax...  62.8 us

profile of v2, /device:TPU:0, one launch (start us, length us, event | category | flops | bytes accessed | tf_op | source)
XLA Modules:
  0.0 174.2 jit_solution(9485197523490392218)
XLA Ops:
  0.7 0.7 iota.19.bias_ref
  1.4 1.0 multiply_sine_fusion
  2.3 3.0 %shard_map.154 = (bf16[1024,256]{1,0:T(8,128)(2,1)}, bf16[1024,256]{1,0:T(8,128)(2,1)}) custom-call(s32[1,8]{1,0:T(1,128)} %table_ref.1, bf16[1,2048,256]{2,1,0:T(8,128)(2,1)} %cache_key_ref.1, bf16[1,2048,256]{2,1,0:T(8,128)(2,1)} %cache_value_ref.1), custom_call_target="tpu_custom_call" | custom-call | tf_op jit(solution)/shard_map/pallas_call | solution.py:390
  5.4 104.3 %shard_map.155 = (bf16[96,4096]{1,0:T(8,128)(2,1)}, bf16[96,128]{1,0:T(8,128)(2,1)}, bf16[128,1024]{1,0:T(8,128)(2,1)}) custom-call(bf16[128,4096]{1,0:T(8,128)(2,1)} %tokens_ref.1, f32[1,4096]{1,0:T(1,128)} %bitcast.9, f32[128,64]{1,0:T(8,128)} %get-tuple-element.16.cosine_ref, f32[128,64]{1,0:T(8,128)} %get-tuple-element.15.sine_ref, ...), custom_call_target="tpu_custom_call" | custom-call | tf_op jit(solution)/shard_map/pallas_call | solution.py:1018
  109.6 62.8 %shard_map.156 = bf16[128,1024]{1,0:T(8,128)(2,1)} custom-call(bf16[96,4096]{1,0:T(8,128)(2,1)} %get-tuple-element.12.buffer_ref, bf16[1,1600,4096]{2,1,0:T(8,128)(2,1)} %bitcast.13, bf16[1,1600,4096]{2,1,0:T(8,128)(2,1)} %bitcast.14, bf16[1,1600,4096]{2,1,0:T(8,128)(2,1)} %down_ref.1, bf16[96,128]{1,0:T(8,128)(2,1)} %get-tuple-element.13.combine_ref, ...), custom_call_target="tpu_custom_call" | custom-call | flops 15099494400 | bytes 39321600 | tf_op jit(solution)/shard_map/pallas_call | solution.py:325
  172.5 1.7 copy.19
  (3 shorter events, 0.0 us)
